TPU v7x, 256 devices: a whole 4x4x8 slice. The times are simulated.
256 devices in a mesh: dp: 32 (over z_lo, y, core), rows: 8 (over x, z_hi).
Axes of the slice: x: 4, y: 4, z: 8 (z_hi: 2, z_lo: 4; z = z_hi * 4 + z_lo), core: 2. Of those that a mesh axis runs over, the one named last changes fastest.
Arguments:
- act_codes: bfloat16 [32, 32, 32, 704], P('dp', 'rows'), may hold values from -6 to 6
- act_exponents: int32 [32, 32, 32, 22], P('dp', 'rows'), may hold values from -5 to 1
- grad_codes: bfloat16 [32, 32, 32, 704], P('dp', 'rows'), may hold values from -6 to 6
- grad_exponents: int32 [32, 32, 32, 22], P('dp', 'rows'), may hold values from -5 to 1
- conv_kernel: float32 [7, 7, 704], replicated, may hold values from -0.875 to 0.875
- conv_bias: float32 [704], replicated, may hold values from -3 to 3
- norm_gain: float32 [704], replicated, may hold values from 0.1 to 1.9
- norm_shift: float32 [704], replicated, may hold values from -2 to 2
- proj_in: bfloat16 [2816, 704], replicated, may hold values from -0.21875 to 0.21875
- proj_bias: float32 [2816], replicated, may hold values from -2 to 2
- response_gain: float32 [2816], replicated, may hold values from -3 to 3
- proj_out: bfloat16 [2816, 704], replicated, may hold values from -0.109375 to 0.109375
Outputs:
- input_grad: bfloat16 [32, 32, 32, 704], P('dp', 'rows')
- proj_in_grad: float32 [2816, 704], P(('dp', 'rows'))
- kernel_grad: float32 [7, 7, 704], replicated
- norm_grads: float32 [2, 704], replicated
- response_grads: float32 [2, 2816], replicated
All inputs are finite; a program needn't handle non-finite values.
Results may differ from a plain program's by a relative error of at most 0.0056.
Values may be sent and summed in bfloat16 or wider, within the bound.
A program may use at most 128 MiB of HBM per device.

v0:
```python
import math

import jax
import jax.numpy as jnp
from jax import lax
from jax.sharding import PartitionSpec as P

NORM_EPSILON = 1e-06
RESPONSE_EPSILON = 1e-06
HALF_ROOT = 0.7071067811865476
NORMAL_PEAK = 0.3989422804014327


def with_halo(x, sides, width):
    for axis, dim in sides:
        peers, length = (lax.axis_size(axis), x.shape[dim])
        up = [(i, (i + 1) % peers) for i in range(peers - 1)]
        down = [(j, i) for i, j in up]
        last = lax.slice_in_dim(x, length - width, length, axis=dim)
        leading = lax.slice_in_dim(x, 0, width, axis=dim)
        before = lax.ppermute(last, axis, up)
        after = lax.ppermute(leading, axis, down)
        x = jnp.concatenate([before, x, after], axis=dim)
    return x


def block_scaled(quantized, exponents):
    array_shape = quantized.shape
    grouped = quantized.astype(jnp.float32).reshape(array_shape[:-1] + (array_shape[-1] // 32, 32))
    scaled = grouped * jnp.exp2(exponents.astype(jnp.float32))[..., None]
    return scaled.reshape(array_shape).astype(jnp.bfloat16)


def depthwise(padded, weights, out_rows, out_columns):
    result = jnp.zeros((out_rows, out_columns, padded.shape[-1]), jnp.float32)
    for tap_row in range(7):
        for tap_column in range(7):
            window = padded[
                tap_row : tap_row + out_rows, tap_column : tap_column + out_columns, :
            ].astype(jnp.float32)
            result = result + window * weights[tap_row, tap_column]
    return result


def kernel_terms(padded, upstream, out_rows, out_columns):
    tap_totals = []
    for tap_row in range(7):
        for tap_column in range(7):
            window = padded[
                tap_row : tap_row + out_rows, tap_column : tap_column + out_columns, :
            ].astype(jnp.float32)
            tap_totals.append(jnp.sum(window * upstream, axis=(0, 1)))
    return jnp.stack(tap_totals).reshape(7, 7, padded.shape[-1])


def shards(
    act_codes,
    act_exponents,
    grad_codes,
    grad_exponents,
    conv_kernel,
    conv_bias,
    norm_gain,
    norm_shift,
    proj_in,
    proj_bias,
    response_gain,
    proj_out,
):
    row_count = act_codes.shape[1]
    column_count = act_codes.shape[2]
    channels = act_codes.shape[3]
    hidden_units = proj_in.shape[0]
    token_count = row_count * column_count
    data_count = lax.axis_size("dp")
    strip_count = lax.axis_size("rows")
    grad_scale = 1.0 / math.sqrt(data_count * strip_count * token_count)
    inputs = block_scaled(act_codes, act_exponents)[0]
    extended = with_halo(inputs, (("rows", 0),), 3)
    padded_in = jnp.pad(extended, ((0, 0), (3, 3), (0, 0)))
    mixed = depthwise(padded_in, conv_kernel, row_count, column_count) + conv_bias
    mixed_flat = mixed.reshape(token_count, channels)
    centered = mixed_flat - jnp.mean(mixed_flat, axis=1, keepdims=True)
    inverse = lax.rsqrt(jnp.mean(centered * centered, axis=1, keepdims=True) + NORM_EPSILON)
    normed = centered * inverse
    normed_in = (normed * norm_gain + norm_shift).astype(jnp.bfloat16)
    preact = (
        lax.dot_general(
            normed_in, proj_in, (((1,), (1,)), ((), ())), preferred_element_type=jnp.float32
        )
        + proj_bias
    )
    cumulative = 0.5 * (1.0 + lax.erf(preact * HALF_ROOT))
    activation = preact * cumulative
    local_squares = jnp.sum(activation * activation, axis=0)
    upstream = block_scaled(grad_codes, grad_exponents)[0].reshape(token_count, channels)
    squares = lax.psum(local_squares, "rows")
    down_grad = lax.dot_general(
        upstream, proj_out, (((1,), (1,)), ((), ())), preferred_element_type=jnp.float32
    )
    local_products = jnp.sum(down_grad * activation, axis=0)
    products = lax.psum(local_products, "rows")
    magnitude = jnp.sqrt(squares + RESPONSE_EPSILON)
    denominator = jnp.mean(magnitude) + RESPONSE_EPSILON
    response = magnitude / denominator
    scaled_products = response_gain * products
    magnitude_grad = scaled_products / denominator - jnp.sum(scaled_products * magnitude) / (
        denominator * denominator * hidden_units
    )
    activation_grad = down_grad * (1.0 + response_gain * response) + activation * (
        magnitude_grad / magnitude
    )
    density = NORMAL_PEAK * jnp.exp(-0.5 * preact * preact)
    preact_grad = (activation_grad * (cumulative + preact * density)).astype(jnp.bfloat16)
    inner_sum = lax.psum_scatter(
        lax.dot_general(
            preact_grad, normed_in, (((0,), (0,)), ((), ())), preferred_element_type=jnp.float32
        ),
        ("dp", "rows"),
        scatter_dimension=0,
        tiled=True,
    )
    normed_grad = jnp.dot(preact_grad, proj_in, preferred_element_type=jnp.float32)
    gain_part = jnp.sum(normed_grad * normed, axis=0)
    shift_part = jnp.sum(normed_grad, axis=0)
    scaled_grad = normed_grad * norm_gain
    mixed_grad = (
        inverse
        * (
            scaled_grad
            - jnp.mean(scaled_grad, axis=1, keepdims=True)
            - normed * jnp.mean(scaled_grad * normed, axis=1, keepdims=True)
        )
    ).astype(jnp.bfloat16)
    mixed_grid = mixed_grad.reshape(row_count, column_count, channels)
    grad_strip = with_halo(mixed_grid, (("rows", 0),), 3)
    grad_padded = jnp.pad(grad_strip, ((0, 0), (3, 3), (0, 0)))
    spread = depthwise(grad_padded, conv_kernel[::-1, ::-1], row_count, column_count)
    input_grad = (
        upstream.reshape(row_count, column_count, channels).astype(jnp.float32) + spread
    ).astype(jnp.bfloat16)[None]
    kernel_part = kernel_terms(padded_in, mixed_grid.astype(jnp.float32), row_count, column_count)
    norm_part = jnp.stack([gain_part, shift_part])
    response_part = jnp.stack([response * local_products, jnp.sum(down_grad, axis=0)])
    kernel_sum, norm_sum, response_sum = lax.psum(
        (kernel_part, norm_part, response_part), ("dp", "rows")
    )
    return (
        input_grad,
        inner_sum * grad_scale,
        kernel_sum * grad_scale,
        norm_sum * grad_scale,
        response_sum * grad_scale,
    )


def solution(mesh):
    placed = (
        P("dp", "rows", None, None),
        P("dp", "rows", None, None),
        P("dp", "rows", None, None),
        P("dp", "rows", None, None),
        P(),
        P(),
        P(),
        P(),
        P(),
        P(),
        P(),
        P(),
    )
    return jax.shard_map(
        shards,
        mesh=mesh,
        in_specs=placed,
        out_specs=(P("dp", "rows", None, None), P(("dp", "rows"), None), P(), P(), P()),
        check_vma=False,
    )
```

profile of v0, /device:TPU:1, one launch (start us, length us, event | category | flops | bytes accessed | tf_op | source)
XLA Modules:
  0.0 398.2 jit_solution(18050940125475015131)
XLA Ops:
  7.2 0.8 exponential_bitcast_fusion
  9.1 9.7 %collective-permute-start = (bf16[3,32,704]{2,1,0:T(8,128)(2,1)S(1)}, bf16[3,32,704]{2,1,0:T(8,128)(2,1)S(1)}, u32[]{:S(2)}, u32[]{:S(2)}) collective-permute-start(bf16[3,32,704]{2,1,0:T(8,128)(2,1)S(1)} %get-tuple-element.124), channel_id=1, source_target_pairs={{0,1},{1,2},{2,3},{3,4},{4,5},{5,6},{6,7},{8,9},{9,10},{10,11},{11... | collective-permute-start | bytes 405512 | tf_op jit(solution)/shard_map/ppermute | solution.py:21
  18.8 1.3 collective-permute-start.1
  21.8 0.8 slice_reduce_fusion.46
  22.6 9.1 %collective-permute-done.1 = bf16[3,32,704]{2,1,0:T(8,128)(2,1)S(1)} collective-permute-done((bf16[3,32,704]{2,1,0:T(8,128)(2,1)S(1)}, bf16[3,32,704]{2,1,0:T(8,128)(2,1)S(1)}, u32[]{:S(2)}, u32[]{:S(2)}) %collective-permute-start.1) | collective-permute-done | bytes 135200 | tf_op jit(solution)/shard_map/ppermute | solution.py:22
  32.1 5.2 %fusion.152 = (f32[4,32]{1,0:T(4,128)S(1)}, f32[4,32,704]{2,1,0:T(8,128)S(1)}) fusion(f32[704]{0:T(1024)S(1)} %copy-done.96, f32[704]{0:T(1024)S(1)} %get-tuple-element.111, bf16[10,38,704]{2,1,0:T(8,128)(2,1)S(1)} %fusion.11, f32[704]{0:T(1024)S(1)} %get-tuple-element.112, f32[704]{0:T(1024)S(1)} %get-tuple-element.65, f32[704]{0:T(1024)S(1)} %get-tuple-element.66, ...), kind=kLoop, calls=%fused_computation.356 | loop fusion | flops 13877120 | bytes 8521728 | tf_op jit(solution)/shard_map/reduce_sum | solution.py:83
  38.0 3.2 convolution_add_fusion
  41.4 3.2 fusion.150
  44.5 45.8 %all-reduce.5 = (f32[2816]{0:T(1024)S(1)}, f32[2816]{0:T(1024)S(1)}) all-reduce(f32[2816]{0:T(1024)S(1)} %get-tuple-element.7, f32[2816]{0:T(1024)S(1)} %get-tuple-element.6), channel_id=1, replica_groups=mesh['dp'=32,'rows'=8] {'rows'}, use_global_device_ids=true, to_apply=%region_3.4 | all-reduce | flops 5632 | bytes 45056 | tf_op jit(solution)/shard_map/psum | solution.py:97
  90.3 0.7 fusion.146
  92.2 2.7 fusion.5
  95.2 1.3 multiply_reduce_fusion.3
  97.2 0.9 fusion.133
  98.1 0.9 fusion.112
  99.0 4.7 %fusion.148 = f32[2816,704]{1,0:T(8,128)} fusion(bf16[128,2816]{1,0:T(8,128)(2,1)S(1)} %fusion.5, f32[128,704]{0,1:T(8,128)S(1)} %copy.34, f32[704]{0:T(1024)S(1)} %copy-done.88, f32[704]{0:T(1024)S(1)} %copy-done.11, f32[128]{0:T(128)S(1)} %copy-done.91, f32[128]{0:T(128)S(1)} %copy-done.94), kind=kOutput, calls=%fused_computation.353 | convolution fusion | flops 507961344 | bytes 9017856 | tf_op jit(solution)/shard_map/dot_general | solution.py:116
  104.9 0.7 reshape.99
  106.8 1.3 collective-permute-start.3
  108.1 7.9 %collective-permute-start.2 = (bf16[3,32,704]{2,1,0:T(8,128)(2,1)S(1)}, bf16[3,32,704]{2,1,0:T(8,128)(2,1)S(1)}, u32[]{:S(2)}, u32[]{:S(2)}) collective-permute-start(bf16[3,32,704]{2,1,0:T(8,128)(2,1)S(1)} %bitcast.84), channel_id=1, source_target_pairs={{0,1},{1,2},{2,3},{3,4},{4,5},{5,6},{6,7},{8,9},{9,10},{10,11},{11... | collective-permute-start | bytes 405512 | tf_op jit(solution)/shard_map/ppermute | solution.py:21
  116.1 83.1 %all-reduce.3 = (f32[2,704]{1,0:T(2,128)S(1)}, f32[2,2816]{1,0:T(2,128)S(1)}) all-reduce(f32[2,704]{1,0:T(2,128)S(1)} %pad_maximum_fusion.5, f32[2,2816]{1,0:T(2,128)S(1)} %pad_maximum_fusion.4), channel_id=1, replica_groups=mesh['dp'=32,'rows'=8] {'dp','rows'}, use_global_device_ids=true, to_apply=%region_63.64 | all-reduce | flops 7040 | bytes 56320 | tf_op jit(solution)/shard_map/psum | solution.py:145
  199.1 0.6 broadcast_multiply_fusion.1
  200.9 4.5 %fusion.144 = bf16[1,4,32,704]{3,2,1,0:T(8,128)(2,1)} fusion(f32[704]{0:T(1024)S(1)} %copy-done.66, bf16[10,38,704]{2,1,0:T(8,128)(2,1)S(1)} %select_maximum_fusion, f32[704]{0:T(1024)S(1)} %get-tuple-element.64, f32[704]{0:T(1024)S(1)} %copy-done.72, f32[704]{0:T(1024)S(1)} %copy-done.50, bf16[3,32,704]{2,1,0:T(8,128)(2,1)S(1)} %collective-permute-done.3, ...), kind=kLoop, calls=%fused_computation.282 | loop fusion | flops 13967360 | bytes 8518400 | tf_op jit(solution)/shard_map/broadcast_in_dim | solution.py:139
  205.5 182.8 %all-reduce.8.cloned.1.call-done = (f32[2816,704]{1,0:T(8,128)}, f32[7,7,704]{2,1,0:T(8,128)}) async-done(((f32[2816,704]{1,0:T(8,128)}, f32[7,7,704]{2,1,0:T(8,128)}), (f32[2816,704]{1,0:T(8,128)}, f32[7,7,704]{2,1,0:T(8,128)})) %all-reduce.8.cloned.1.call-update) | async-done | bytes 8067856
  388.2 1.6 broadcast_multiply_fusion
  389.8 1.5 dynamic-slice_multiply_fusion
  (285 shorter events, 7.0 us)
Async XLA Ops:
  7.2 381.1 %all-reduce.8.cloned.1.call-start = ((), (), s32[]{:S(2)}) async-start(), calls=%async_computation | async-start | bytes 17645568
  9.1 13.4 %collective-permute-start = (bf16[3,32,704]{2,1,0:T(8,128)(2,1)S(1)}, bf16[3,32,704]{2,1,0:T(8,128)(2,1)S(1)}, u32[]{:S(2)}, u32[]{:S(2)}) collective-permute-start(bf16[3,32,704]{2,1,0:T(8,128)(2,1)S(1)} %get-tuple-element.124), channel_id=1, source_target_pairs={{0,1},{1,2},{2,3},{3,4},{4,5},{5,6},{6,7},{8,9},{9,10},{10,11},{11... | collective-permute-start | bytes 405512 | tf_op jit(solution)/shard_map/ppermute | solution.py:21
  18.8 12.9 %collective-permute-start.1 = (bf16[3,32,704]{2,1,0:T(8,128)(2,1)S(1)}, bf16[3,32,704]{2,1,0:T(8,128)(2,1)S(1)}, u32[]{:S(2)}, u32[]{:S(2)}) collective-permute-start(bf16[3,32,704]{2,1,0:T(8,128)(2,1)S(1)} %get-tuple-element.125), channel_id=1, source_target_pairs={{1,0},{2,1},{3,2},{4,3},{5,4},{6,5},{7,6},{9,8},{10,9},{11,10},{12... | collective-permute-start | bytes 405512 | tf_op jit(solution)/shard_map/ppermute | solution.py:22
  105.7 94.9 %copy-start.3 = (bf16[1,4,32,704]{3,2,1,0:T(8,128)(2,1)S(1)}, bf16[1,4,32,704]{3,2,1,0:T(8,128)(2,1)}, u32[]{:S(2)}) copy-start(bf16[1,4,32,704]{3,2,1,0:T(8,128)(2,1)} %copy-done.2) | copy-start | bytes 540676
  105.7 94.9 %copy-start.16 = (f32[704]{0:T(1024)S(1)}, f32[704]{0:T(1024)}, u32[]{:S(2)}) copy-start(f32[704]{0:T(1024)} %copy-done.15) | copy-start | bytes 8452
  105.7 94.9 %copy-start.18 = (f32[704]{0:T(1024)S(1)}, f32[704]{0:T(1024)}, u32[]{:S(2)}) copy-start(f32[704]{0:T(1024)} %copy-done.17) | copy-start | bytes 8452
  105.7 94.9 %copy-start.20 = (f32[704]{0:T(1024)S(1)}, f32[704]{0:T(1024)}, u32[]{:S(2)}) copy-start(f32[704]{0:T(1024)} %copy-done.19) | copy-start | bytes 8452
  105.7 94.9 %copy-start.22 = (f32[704]{0:T(1024)S(1)}, f32[704]{0:T(1024)}, u32[]{:S(2)}) copy-start(f32[704]{0:T(1024)} %copy-done.21) | copy-start | bytes 8452
  105.7 94.9 %copy-start.24 = (f32[704]{0:T(1024)S(1)}, f32[704]{0:T(1024)}, u32[]{:S(2)}) copy-start(f32[704]{0:T(1024)} %copy-done.23) | copy-start | bytes 8452
  105.7 94.9 %copy-start.26 = (f32[704]{0:T(1024)S(1)}, f32[704]{0:T(1024)}, u32[]{:S(2)}) copy-start(f32[704]{0:T(1024)} %copy-done.25) | copy-start | bytes 8452
  105.7 94.9 %copy-start.28 = (f32[704]{0:T(1024)S(1)}, f32[704]{0:T(1024)}, u32[]{:S(2)}) copy-start(f32[704]{0:T(1024)} %copy-done.27) | copy-start | bytes 8452
  105.7 94.9 %copy-start.30 = (f32[704]{0:T(1024)S(1)}, f32[704]{0:T(1024)}, u32[]{:S(2)}) copy-start(f32[704]{0:T(1024)} %copy-done.29) | copy-start | bytes 8452
  105.7 94.9 %copy-start.32 = (f32[704]{0:T(1024)S(1)}, f32[704]{0:T(1024)}, u32[]{:S(2)}) copy-start(f32[704]{0:T(1024)} %copy-done.31) | copy-start | bytes 8452
  105.8 94.9 %copy-start.34 = (f32[704]{0:T(1024)S(1)}, f32[704]{0:T(1024)}, u32[]{:S(2)}) copy-start(f32[704]{0:T(1024)} %copy-done.33) | copy-start | bytes 8452
  105.8 94.9 %copy-start.36 = (f32[704]{0:T(1024)S(1)}, f32[704]{0:T(1024)}, u32[]{:S(2)}) copy-start(f32[704]{0:T(1024)} %copy-done.35) | copy-start | bytes 8452
  105.8 94.9 %copy-start.38 = (f32[704]{0:T(1024)S(1)}, f32[704]{0:T(1024)}, u32[]{:S(2)}) copy-start(f32[704]{0:T(1024)} %copy-done.37) | copy-start | bytes 8452
  105.8 94.9 %copy-start.40 = (f32[704]{0:T(1024)S(1)}, f32[704]{0:T(1024)}, u32[]{:S(2)}) copy-start(f32[704]{0:T(1024)} %copy-done.39) | copy-start | bytes 8452
  105.8 94.9 %copy-start.42 = (f32[704]{0:T(1024)S(1)}, f32[704]{0:T(1024)}, u32[]{:S(2)}) copy-start(f32[704]{0:T(1024)} %copy-done.41) | copy-start | bytes 8452
  105.8 94.9 %copy-start.44 = (f32[704]{0:T(1024)S(1)}, f32[704]{0:T(1024)}, u32[]{:S(2)}) copy-start(f32[704]{0:T(1024)} %copy-done.43) | copy-start | bytes 8452
  105.8 94.9 %copy-start.46 = (f32[704]{0:T(1024)S(1)}, f32[704]{0:T(1024)}, u32[]{:S(2)}) copy-start(f32[704]{0:T(1024)} %copy-done.45) | copy-start | bytes 8452
  105.8 94.9 %copy-start.48 = (f32[704]{0:T(1024)S(1)}, f32[704]{0:T(1024)}, u32[]{:S(2)}) copy-start(f32[704]{0:T(1024)} %copy-done.47) | copy-start | bytes 8452
  105.8 94.9 %copy-start.50 = (f32[704]{0:T(1024)S(1)}, f32[704]{0:T(1024)}, u32[]{:S(2)}) copy-start(f32[704]{0:T(1024)} %copy-done.49) | copy-start | bytes 8452
  106.8 93.6 %collective-permute-start.3 = (bf16[3,32,704]{2,1,0:T(8,128)(2,1)S(1)}, bf16[3,32,704]{2,1,0:T(8,128)(2,1)S(1)}, u32[]{:S(2)}, u32[]{:S(2)}) collective-permute-start(bf16[3,32,704]{2,1,0:T(8,128)(2,1)S(1)} %bitcast.85), channel_id=1, source_target_pairs={{1,0},{2,1},{3,2},{4,3},{5,4},{6,5},{7,6},{9,8},{10,9},{11,10},{12... | collective-permute-start | bytes 405512 | tf_op jit(solution)/shard_map/ppermute | solution.py:22
  108.1 92.3 %collective-permute-start.2 = (bf16[3,32,704]{2,1,0:T(8,128)(2,1)S(1)}, bf16[3,32,704]{2,1,0:T(8,128)(2,1)S(1)}, u32[]{:S(2)}, u32[]{:S(2)}) collective-permute-start(bf16[3,32,704]{2,1,0:T(8,128)(2,1)S(1)} %bitcast.84), channel_id=1, source_target_pairs={{0,1},{1,2},{2,3},{3,4},{4,5},{5,6},{6,7},{8,9},{9,10},{10,11},{11... | collective-permute-start | bytes 405512 | tf_op jit(solution)/shard_map/ppermute | solution.py:21
  (78 other events, 2368.6 us)
Sparse Core Ops, SparseCore 0:
  105.8 282.3 all-reduce.7
where the time goes:
time: 399 us; the launch traced here: 398 us
  waiting for transfers between devices  192 us (48%)
  blocking collectives  129 us (32%)
  other arithmetic  21.5 us (5%)
  starting transfers between devices  20.2 us (5%)
  between operations  17.2 us (4%)
  matrix products  12.3 us (3%)
  local copies, waits for them, and re-layouts  6.24 us (2%)
    unnamed x2, waiting for transfers between devices  183 us
    psum x1, blocking collectives, shards(): lax.psum((kernel_part, norm_part, response_part), ('dp', 'rows'))  83.1 us
    psum x1, blocking collectives, shards(): squares = lax.psum(local_squares, 'rows')  45.8 us
    ppermute x2, starting transfers between devices, with_halo(): before = lax.ppermute(last, axis, up)  17.6 us
    ppermute x2, waiting for transfers between devices, with_halo(): after = lax.ppermute(leading, axis, down)  9.1 us
  transfers between devices with their start and end apart: 5, of which 2 were waited for; matrix products, arithmetic and copies ran while one was open for 2% of the time, Pallas kernels for 0%

commit v1 on v0

v1 whole, which is shorter than its diff:
```python
import math

import jax
import jax.numpy as jnp
from jax import lax
from jax.experimental import pallas as pl
from jax.experimental.pallas import tpu as pltpu
from jax.sharding import PartitionSpec as P

NORM_EPSILON = 1e-06
RESPONSE_EPSILON = 1e-06
HALF_ROOT = 0.7071067811865476
NORMAL_PEAK = 0.3989422804014327

C = 704
CP = 768
CT = CP // 128
H = 2816
HT = H // 128
R = 4
W = 32
T = R * W
S = H // 8
B = S // 4
U = B // 8
F32 = jnp.float32
BF16 = jnp.bfloat16

ALPHA = (
    0.00022905065861350646,
    0.0034082910107109506,
    0.050955695062380861,
    0.18520832239976145,
    1.128379143519084,
)
BETA = (
    -1.1791602954361697e-7,
    0.000023547966471313185,
    0.0010179625278914885,
    0.014070470171167667,
    0.11098505178285362,
    0.49746925110067538,
    1.0,
)


def erf(v):
    v = jnp.clip(v, -3.7439211627767994, 3.7439211627767994)
    s = v * v
    top = jnp.full_like(s, ALPHA[0])
    for c in ALPHA[1:]:
        top = top * s + c
    low = jnp.full_like(s, BETA[0])
    for c in BETA[1:]:
        low = low * s + c
    return v * top / low


def lanes(i, n=128):
    return pl.ds(pl.multiple_of(i * n, n), n)


def moved(v, d):
    if d == 0:
        return v
    w = lax.broadcasted_iota(jnp.int32, v.shape, 0) + d
    return jnp.where((w >= 0) & (w < W), pltpu.roll(v, (-d) % W, 0), 0.0)


def depthwise(rows, weight):
    out = [None] * R
    for b in range(7):
        for r in range(R):
            acc = rows[r] * weight(0, b)
            for a in range(1, 7):
                acc = acc + rows[r + a] * weight(a, b)
            acc = moved(acc, b - 3)
            out[r] = acc if out[r] is None else out[r] + acc
    return out


def body(
    act_ref, aexp_ref, grad_ref, gexp_ref, ck_ref, cb_ref, gain_ref, shift_ref,
    win_hbm, pb_ref, rg_ref, wout_hbm,
    ig_ref, dw_ref, kg_ref, ng_ref, rp_ref,
    win, wout, ckp, prm, sx, su, xs, up, mg, mx, normed, inv, ni, niall,
    act, gp, dg, pg, pgt, pgr, stq, stp, rq, rp, coef, dwf, dwb, xr, zacc, zs, zr,
    ngb, xf, red, redr, ysum, yr, zsum, zar, fin, og,
    wsem, bsem, ssend, srecv, hsend, hrecv, gsend, grecv, nsend, nrecv, fsend, frecv,
    psend, precv, lsem, xsend, xrecv, zsend, zrecv, rsend, rrecv, ysend, yrecv,
    asend, arecv, qsend, qrecv, osend, orecv,
):
    dp, rw = lax.axis_index("dp"), lax.axis_index("rows")
    core = lax.rem(dp, 2)
    y = lax.rem(lax.div(dp, 2), 4)
    zl = lax.div(dp, 8)
    x = lax.div(rw, 2)
    zh = lax.rem(rw, 2)
    z = zh * 4 + zl
    gx = 2 * x + core
    gy = 2 * y + core

    def dev(x=x, y=y, zl=zl, zh=zh, core=core):
        return {"dp": (zl * 4 + y) * 2 + core, "rows": x * 2 + zh}

    def in_gx(i):
        m = lax.rem(gx + i, 8)
        return dev(x=lax.div(m, 2), core=lax.rem(m, 2))

    def in_gy(i):
        m = lax.rem(gy + i, 8)
        return dev(y=lax.div(m, 2), core=lax.rem(m, 2)), m

    def in_z(i):
        m = lax.rem(z + i, 8)
        return dev(zl=lax.rem(m, 4), zh=lax.div(m, 4))

    def same(d):
        return (d["dp"] == dp) & (d["rows"] == rw)

    swap = core != zh
    swap_dev = dev(zh=1 - zh, core=1 - core)
    sib = dev(core=1 - core)

    def owner(g):
        return dev(
            x=g // 2,
            y=2 * core + lax.div(x, 2),
            zl=y,
            zh=jnp.int32(g % 2),
            core=lax.rem(x, 2),
        )

    def source(k):
        return dev(
            x=2 * lax.rem(y, 2) + core,
            y=zl,
            zl=jnp.int32(k % 4),
            zh=jnp.int32(k // 4),
            core=lax.div(y, 2),
        )

    def remote(src, dst, send, recv, to):
        return pltpu.make_async_remote_copy(
            src_ref=src, dst_ref=dst, send_sem=send, recv_sem=recv,
            device_id=to, device_id_type=pl.DeviceIdType.MESH,
        )

    win_copy = pltpu.make_async_copy(win_hbm, win.at[pl.ds(0, C)], wsem.at[0])
    wout_copy = pltpu.make_async_copy(wout_hbm, wout.at[pl.ds(0, C)], wsem.at[1])
    win_copy.start()
    wout_copy.start()

    barrier = pltpu.get_barrier_semaphore()

    def greet(d):
        pl.semaphore_signal(
            barrier, inc=1, device_id=d, device_id_type=pl.DeviceIdType.MESH
        )

    @pl.when(swap)
    def _():
        greet(swap_dev)

    for i in range(1, 8):
        greet(in_gx(i))
    for i in range(1, 8):
        d, m = in_gy(i)
        greet(d)
    for i in range(1, 8):
        greet(in_z(i))
    guests = 21 + jnp.where(swap, 1, 0)
    for g in range(8):
        for d in (owner(g), source(g)):
            other = jnp.logical_not(same(d))
            guests = guests + jnp.where(other, 1, 0)

            @pl.when(other)
            def _():
                greet(d)

    member = lax.broadcasted_iota(jnp.int32, (C // 32, CP), 1) // 32
    block = lax.broadcasted_iota(jnp.int32, (C // 32, CP), 0)
    spread = jnp.where(member == block, 1.0, 0.0).astype(BF16)

    def scaled(codes, exps, out):
        for r in range(R):
            power = jnp.exp2(exps[:, r, :].astype(F32)).astype(BF16)
            full = lax.dot_general(
                power, spread, (((0,), (0,)), ((), ())), preferred_element_type=F32
            )
            out[r, :, C - 64 : CP] = jnp.zeros((W, CP - C + 64), BF16)
            out[r, :, 0:C] = (codes[r].astype(F32) * full[:, 0:C]).astype(BF16)

    scaled(act_ref, aexp_ref, sx)

    pl.semaphore_wait(barrier, guests)

    swap_x = remote(sx, xs.at[pl.ds(3, R)], ssend.at[0], srecv.at[0], swap_dev)
    swap_u = remote(su, up, ssend.at[1], srecv.at[1], swap_dev)

    @pl.when(swap)
    def _():
        swap_x.start()

    scaled(grad_ref, gexp_ref, su)

    @pl.when(swap)
    def _():
        swap_u.start()

    @pl.when(jnp.logical_not(swap))
    def _():
        xs[3 : 3 + R] = sx[...]
        up[...] = su[...]

    ckp[...] = jnp.zeros_like(ckp)
    prm[...] = jnp.zeros_like(prm)
    ckp[:, 0:7, 0:C] = ck_ref[...]
    prm[0:1, 0:C] = cb_ref[...]
    prm[1:2, 0:C] = gain_ref[...]
    prm[2:3, 0:C] = shift_ref[...]
    win[C:CP, :] = jnp.zeros((CP - C, H), BF16)
    wout[C:CP, :] = jnp.zeros((CP - C, H), BF16)
    first, last = gx == 0, gx == 7

    @pl.when(first)
    def _():
        xs[0:3] = jnp.zeros((3, W, CP), BF16)
        mg[0:3] = jnp.zeros((3, W, CP), BF16)

    @pl.when(last)
    def _():
        xs[7:10] = jnp.zeros((3, W, CP), BF16)
        mg[7:10] = jnp.zeros((3, W, CP), BF16)

    below, above = lax.rem(gx + 1, 8), lax.rem(gx + 7, 8)
    below_dev = dev(x=lax.div(below, 2), core=lax.rem(below, 2))
    above_dev = dev(x=lax.div(above, 2), core=lax.rem(above, 2))

    def halo(buf, base):
        down = remote(buf.at[pl.ds(4, 3)], buf.at[pl.ds(0, 3)],
                      hsend.at[base], hrecv.at[base], below_dev)
        upward = remote(buf.at[pl.ds(3, 3)], buf.at[pl.ds(7, 3)],
                        hsend.at[base + 1], hrecv.at[base + 1], above_dev)

        def start():
            @pl.when(jnp.logical_not(last))
            def _():
                down.start()

            @pl.when(jnp.logical_not(first))
            def _():
                upward.start()

        def arrive():
            @pl.when(jnp.logical_not(first))
            def _():
                down.wait_recv()

            @pl.when(jnp.logical_not(last))
            def _():
                upward.wait_recv()

        def finish():
            @pl.when(jnp.logical_not(last))
            def _():
                down.wait_send()

            @pl.when(jnp.logical_not(first))
            def _():
                upward.wait_send()

        return start, arrive, finish

    @pl.when(swap)
    def _():
        swap_x.wait_recv()

    x_start, x_arrive, x_finish = halo(xs, 0)
    x_start()
    x_arrive()

    def conv_tile(t, _):
        at = lanes(t)
        rows = [xs[i, :, at].astype(F32) for i in range(R + 6)]
        out = depthwise(rows, lambda a, b: ckp[a, b : b + 1, at])
        for r in range(R):
            mx[pl.ds(r * W, W), at] = out[r] + prm[0:1, at]
        return 0

    lax.fori_loop(0, CT, conv_tile, 0)

    inside = lax.broadcasted_iota(jnp.int32, (W, CP), 1) < C

    def norm_block(r, _):
        at = pl.ds(pl.multiple_of(r * W, W), W)
        v = mx[at, :]
        centered = jnp.where(inside, v - jnp.sum(v, axis=1, keepdims=True) / C, 0.0)
        var = jnp.sum(centered * centered, axis=1, keepdims=True) / C
        inverse = lax.rsqrt(var + NORM_EPSILON)
        n = centered * inverse
        normed[at, :] = n
        inv[at, :] = jnp.broadcast_to(inverse, (W, 128))
        ni[at, :] = (n * prm[1:2, :] + prm[2:3, :]).astype(BF16)
        return 0

    lax.fori_loop(0, R, norm_block, 0)

    ni_copies = []
    for i in range(1, 4):
        to = dev(y=lax.rem(y + i, 4))
        ni_copies.append(
            remote(ni, niall.at[gy], nsend.at[i - 1], nrecv.at[i - 1], to)
        )
    for c in ni_copies:
        c.start()
    niall[gy] = ni[...]

    stq[...] = jnp.zeros_like(stq)
    stp[...] = jnp.zeros_like(stp)
    red[...] = jnp.zeros_like(red)
    win_copy.wait()

    def active(i, _):
        at = lanes(i, 256)
        p = jnp.dot(ni[...], win[:, at], preferred_element_type=F32) + pb_ref[:, at]
        phi = 0.5 * (1.0 + erf(p * HALF_ROOT))
        v = p * phi
        act[:, at] = v
        gp[:, at] = phi + p * (NORMAL_PEAK * jnp.exp(-0.5 * p * p))
        s = jnp.sum(v * v, axis=0, keepdims=True)
        stq[pl.ds(2 * i, 1), :] = s[:, 0:128]
        stq[pl.ds(2 * i + 1, 1), :] = s[:, 128:256]
        return 0

    lax.fori_loop(0, HT // 2, active, 0)

    def to_group(src, dst, send, recv):
        return [
            remote(src, dst.at[gx], send.at[i - 1], recv.at[i - 1], in_gx(i))
            for i in range(1, 8)
        ]

    q_copies = to_group(stq, rq, gsend.at[0], grecv.at[0])
    for c in q_copies:
        c.start()
    rq[gx] = stq[...]

    @pl.when(swap)
    def _():
        swap_u.wait_recv()

    wout_copy.wait()
    uf = up[...].reshape(T, CP)

    def downward(i, _):
        at = lanes(i, 256)
        d = jnp.dot(uf, wout[:, at], preferred_element_type=F32)
        dg[:, at] = d
        s = jnp.sum(d * act[:, at], axis=0, keepdims=True)
        stp[pl.ds(2 * i, 1), :] = s[:, 0:128]
        stp[pl.ds(2 * i + 1, 1), :] = s[:, 128:256]
        e = jnp.sum(d, axis=0, keepdims=True)
        red[pl.ds(360 + 2 * i, 1), :] = e[:, 0:128]
        red[pl.ds(361 + 2 * i, 1), :] = e[:, 128:256]
        return 0

    lax.fori_loop(0, HT // 2, downward, 0)
    p_copies = to_group(stp, rp, gsend.at[1], grecv.at[1])
    for c in p_copies:
        c.start()
    rp[gx] = stp[...]

    for c in q_copies:
        c.wait_recv()
    squares = rq[0, 0:HT]
    for i in range(1, 8):
        squares = squares + rq[i, 0:HT]
    magnitude = jnp.sqrt(squares + RESPONSE_EPSILON)
    denominator = jnp.sum(magnitude) / H + RESPONSE_EPSILON
    response = magnitude / denominator
    coef[0, 0:HT] = 1.0 + rg_ref[...] * response
    red[336 : 336 + HT] = response * stp[0:HT]
    for c in p_copies:
        c.wait_recv()
    products = rp[0, 0:HT]
    for i in range(1, 8):
        products = products + rp[i, 0:HT]
    scaled_products = rg_ref[...] * products
    magnitude_grad = scaled_products / denominator - jnp.sum(
        scaled_products * magnitude
    ) / (denominator * denominator * H)
    coef[1, 0:HT] = magnitude_grad / magnitude

    def preact(i, _):
        at = lanes(i)
        a = coef[0, pl.ds(i, 1), :]
        b = coef[1, pl.ds(i, 1), :]
        g = (dg[:, at] * a + act[:, at] * b) * gp[:, at]
        pg[:, at] = g.astype(BF16)
        pgt[lanes(i), :] = g.T.astype(BF16)
        return 0

    lax.fori_loop(0, HT, preact, 0)

    own = pl.ds(pl.multiple_of(gy * 128, 128), 128)
    a_copies = []
    for i in range(1, 8):
        to, m = in_gy(i)
        piece = pgt.at[pl.ds(pl.multiple_of(m * S, 32), S)]
        a_copies.append(
            remote(piece, pgr.at[:, own], psend.at[i - 1], precv.at[i - 1], to)
        )
    for c in a_copies:
        c.start()
    pgr[:, own] = pgt[pl.ds(pl.multiple_of(gy * S, 32), S), :]

    for c in ni_copies:
        c.wait_recv()
    f_copies = []
    for k in range(4):
        piece = niall.at[2 * k + core]
        f_copies.append(remote(piece, piece, fsend.at[k], frecv.at[k], sib))
    for c in f_copies:
        c.start()

    ngb[...] = lax.dot_general(
        pg[...], win[...], (((1,), (1,)), ((), ())), preferred_element_type=F32
    )

    def norm_grad(r, sums):
        at = pl.ds(pl.multiple_of(r * W, W), W)
        g = ngb[at, :]
        n = normed[at, :]
        gn = g * n
        s = g * prm[1:2, :]
        m1 = jnp.sum(s, axis=1, keepdims=True) / C
        m2 = jnp.sum(s * n, axis=1, keepdims=True) / C
        v = inv[at, :][:, 0:1] * (s - m1 - n * m2)
        mg[3 + r] = jnp.where(inside, v, 0.0).astype(BF16)
        return (
            sums[0] + jnp.sum(gn, axis=0, keepdims=True),
            sums[1] + jnp.sum(g, axis=0, keepdims=True),
        )

    zero = jnp.zeros((1, CP), F32)
    gain_part, shift_part = lax.fori_loop(0, R, norm_grad, (zero, zero))
    m_start, m_arrive, m_finish = halo(mg, 2)
    m_start()

    def kernel_tile(t, _):
        at = lanes(t)
        for i in range(R + 6):
            xf[i] = xs[i, :, at].astype(F32)
        g = [mg[3 + r, :, at].astype(F32) for r in range(R)]
        base = t * 56
        for b in range(7):
            gs = [moved(v, 3 - b) for v in g]
            for a in range(7):
                s = xf[a] * gs[0]
                for r in range(1, R):
                    s = s + xf[a + r] * gs[r]
                red[pl.ds(base + a * 8 + b, 1), :] = jnp.sum(s, axis=0, keepdims=True)
        return 0

    lax.fori_loop(0, CT, kernel_tile, 0)
    for t in range(CT):
        red[56 * t + 7 : 56 * t + 8, :] = gain_part[:, 128 * t : 128 * t + 128]
        red[56 * t + 15 : 56 * t + 16, :] = shift_part[:, 128 * t : 128 * t + 128]

    def share(m):
        return pl.ds(pl.multiple_of(m * 48, 8), 48)

    r_copies = []
    for i in range(1, 8):
        m = lax.rem(gx + i, 8)
        r_copies.append(
            remote(red.at[share(m)], redr.at[gx], rsend.at[i - 1], rrecv.at[i - 1], in_gx(i))
        )
    for c in r_copies:
        c.start()
    redr[gx] = red[share(gx), :]

    for c in a_copies:
        c.wait_recv()
    for c in f_copies:
        c.wait_recv()
    dwf[S : S + 8, :] = jnp.zeros((8, CP), F32)
    dwf[0:S, :] = jnp.dot(
        pgr[...], niall[...].reshape(8 * T, CP), preferred_element_type=F32
    )
    for k in range(4):
        dwb[k] = dwf[B * k : B * k + 96, :].astype(BF16)
    x_copies = []
    for i in range(1, 4):
        k = lax.rem(x + i, 4)
        x_copies.append(
            remote(dwb.at[k], xr.at[i - 1], xsend.at[i - 1], xrecv.at[i - 1], dev(x=k))
        )
    for c in x_copies:
        c.start()

    m_arrive()

    def back_tile(t, _):
        at = lanes(t)
        rows = [mg[i, :, at].astype(F32) for i in range(R + 6)]
        out = depthwise(rows, lambda a, b: ckp[6 - a, 6 - b : 7 - b, at])
        for r in range(R):
            sx[r, :, at] = (out[r] + up[r, :, at].astype(F32)).astype(BF16)
        return 0

    @pl.when(swap)
    def _():
        swap_x.wait_send()

    lax.fori_loop(0, CT, back_tile, 0)
    og[...] = sx[:, :, 0:C]
    o_copy = remote(og, ig_ref, osend.at[0], orecv.at[0], swap_dev)
    o_local = pltpu.make_async_copy(og, ig_ref, lsem.at[0])

    @pl.when(swap)
    def _():
        o_copy.start()

    @pl.when(jnp.logical_not(swap))
    def _():
        o_local.start()

    for c in r_copies:
        c.wait_recv()
    total = redr[0]
    for i in range(1, 8):
        total = total + redr[i]
    ysum[...] = total
    y_copies = [
        remote(ysum, yr.at[y], ysend.at[i - 1], yrecv.at[i - 1], dev(y=lax.rem(y + i, 4)))
        for i in range(1, 4)
    ]
    for c in y_copies:
        c.start()
    yr[y] = total

    for c in x_copies:
        c.wait_recv()
    zacc[...] = dwf[pl.ds(pl.multiple_of(x * B, 8), 96), :]
    zacc[...] = (
        zacc[...] + xr[0].astype(F32) + xr[1].astype(F32) + xr[2].astype(F32)
    )
    for g in range(8):
        zs[g] = zacc[U * g : U * g + 16, :].astype(BF16)
    z_copies = [
        remote(zs.at[g], zr.at[z], zsend.at[g], zrecv.at[z], owner(g)) for g in range(8)
    ]
    for g in range(8):
        me = same(owner(g))

        @pl.when(jnp.logical_not(me))
        def _():
            z_copies[g].start()

        @pl.when(me)
        def _():
            zr[z] = zs[g]

    for c in y_copies:
        c.wait_recv()
    total = yr[0] + yr[1] + yr[2] + yr[3]
    zsum[...] = total
    s_copies = [
        remote(zsum, zar.at[z], asend.at[i - 1], arecv.at[i - 1], in_z(i))
        for i in range(1, 8)
    ]
    for c in s_copies:
        c.start()
    zar[z] = total

    scale = 1.0 / math.sqrt(32.0 * 32.0 * 32.0)
    for c in s_copies:
        c.wait_recv()
    total = zar[0]
    for i in range(1, 8):
        total = total + zar[i]
    fin[share(gx), :] = total * scale
    l_copies = [
        remote(fin.at[share(gx)], fin.at[share(gx)], qsend.at[i - 1], qrecv.at[i - 1], in_gx(i))
        for i in range(1, 8)
    ]
    for c in l_copies:
        c.start()

    for k in range(8):
        d = source(k)
        got = remote(zs.at[0], zr.at[k], zsend.at[0], zrecv.at[k], d)

        @pl.when(jnp.logical_not(same(d)))
        def _():
            got.wait_recv()

    total = zr[0].astype(F32)
    for k in range(1, 8):
        total = total + zr[k].astype(F32)
    dw_ref[...] = total[0:U, 0:C] * scale

    for c in l_copies:
        c.wait_recv()
    for t in range(CT):
        a0, n = 128 * t, min(128, C - 128 * t)
        for a in range(7):
            row = 56 * t + 8 * a
            kg_ref[a, :, a0 : a0 + n] = fin[row : row + 7, 0:n]
        ng_ref[0:1, a0 : a0 + n] = fin[56 * t + 7 : 56 * t + 8, 0:n]
        ng_ref[1:2, a0 : a0 + n] = fin[56 * t + 15 : 56 * t + 16, 0:n]
    for i in range(HT):
        rp_ref[0:1, 128 * i : 128 * i + 128] = fin[336 + i : 337 + i, :]
        rp_ref[1:2, 128 * i : 128 * i + 128] = fin[360 + i : 361 + i, :]

    x_finish()
    m_finish()

    @pl.when(swap)
    def _():
        swap_u.wait_send()
        o_copy.wait_send()
        o_copy.wait_recv()

    @pl.when(jnp.logical_not(swap))
    def _():
        o_local.wait()

    for c in (
        ni_copies + q_copies + p_copies + a_copies + f_copies
        + r_copies + x_copies + y_copies + s_copies + l_copies
    ):
        c.wait_send()
    for g in range(8):

        @pl.when(jnp.logical_not(same(owner(g))))
        def _():
            z_copies[g].wait_send()


def shards(
    act_codes, act_exponents, grad_codes, grad_exponents, conv_kernel, conv_bias,
    norm_gain, norm_shift, proj_in, proj_bias, response_gain, proj_out,
):
    vmem = pl.BlockSpec(memory_space=pltpu.VMEM)
    hbm = pl.BlockSpec(memory_space=pl.ANY)
    dma = pltpu.SemaphoreType.DMA
    scratch = [
        pltpu.VMEM((CP, H), BF16),
        pltpu.VMEM((CP, H), BF16),
        pltpu.VMEM((7, 8, CP), F32),
        pltpu.VMEM((8, CP), F32),
        pltpu.VMEM((R, W, CP), BF16),
        pltpu.VMEM((R, W, CP), BF16),
        pltpu.VMEM((R + 6, W, CP), BF16),
        pltpu.VMEM((R, W, CP), BF16),
        pltpu.VMEM((R + 6, W, CP), BF16),
        pltpu.VMEM((T, CP), F32),
        pltpu.VMEM((T, CP), F32),
        pltpu.VMEM((T, 128), F32),
        pltpu.VMEM((T, CP), BF16),
        pltpu.VMEM((8, T, CP), BF16),
        pltpu.VMEM((T, H), F32),
        pltpu.VMEM((T, H), F32),
        pltpu.VMEM((T, H), F32),
        pltpu.VMEM((T, H), BF16),
        pltpu.VMEM((H, T), BF16),
        pltpu.VMEM((S, 8 * T), BF16),
        pltpu.VMEM((24, 128), F32),
        pltpu.VMEM((24, 128), F32),
        pltpu.VMEM((8, 24, 128), F32),
        pltpu.VMEM((8, 24, 128), F32),
        pltpu.VMEM((2, 24, 128), F32),
        pltpu.VMEM((S + 8, CP), F32),
        pltpu.VMEM((4, 96, CP), BF16),
        pltpu.VMEM((3, 96, CP), BF16),
        pltpu.VMEM((96, CP), F32),
        pltpu.VMEM((8, 16, CP), BF16),
        pltpu.VMEM((8, 16, CP), BF16),
        pltpu.VMEM((T, CP), F32),
        pltpu.VMEM((R + 6, W, 128), F32),
        pltpu.VMEM((384, 128), F32),
        pltpu.VMEM((8, 48, 128), F32),
        pltpu.VMEM((48, 128), F32),
        pltpu.VMEM((4, 48, 128), F32),
        pltpu.VMEM((48, 128), F32),
        pltpu.VMEM((8, 48, 128), F32),
        pltpu.VMEM((384, 128), F32),
        pltpu.VMEM((R, W, C), BF16),
        dma((2,)),
        dma((1,)),
        dma((2,)), dma((2,)),
        dma((4,)), dma((4,)),
        dma((2, 7)), dma((2, 7)),
        dma((3,)), dma((3,)),
        dma((4,)), dma((4,)),
        dma((7,)), dma((7,)),
        dma((1,)),
        dma((3,)), dma((3,)),
        dma((8,)), dma((8,)),
        dma((7,)), dma((7,)),
        dma((3,)), dma((3,)),
        dma((7,)), dma((7,)),
        dma((7,)), dma((7,)),
        dma((1,)), dma((1,)),
    ]
    outs = pl.pallas_call(
        body,
        out_shape=(
            jax.ShapeDtypeStruct((R, W, C), BF16),
            jax.ShapeDtypeStruct((U, C), F32),
            jax.ShapeDtypeStruct((7, 7, C), F32),
            jax.ShapeDtypeStruct((2, C), F32),
            jax.ShapeDtypeStruct((2, H), F32),
        ),
        in_specs=[vmem] * 8 + [hbm, vmem, vmem, hbm],
        out_specs=(hbm, vmem, vmem, vmem, vmem),
        scratch_shapes=scratch,
        compiler_params=pltpu.CompilerParams(
            collective_id=0, has_side_effects=True, vmem_limit_bytes=56 * 1024 * 1024
        ),
    )(
        act_codes[0],
        act_exponents[0].transpose(2, 0, 1),
        grad_codes[0],
        grad_exponents[0].transpose(2, 0, 1),
        conv_kernel,
        conv_bias.reshape(1, C),
        norm_gain.reshape(1, C),
        norm_shift.reshape(1, C),
        proj_in.T,
        proj_bias.reshape(1, H),
        response_gain.reshape(HT, 128),
        proj_out.T,
    )
    return (outs[0][None],) + tuple(outs[1:])


def solution(mesh):
    strips = P("dp", "rows", None, None)
    return jax.shard_map(
        shards,
        mesh=mesh,
        in_specs=(strips,) * 4 + (P(),) * 8,
        out_specs=(strips, P(("dp", "rows"), None), P(), P(), P()),
        check_vma=False,
    )
```

time: 399 us -> 94.9 us (0.24)
  waiting for transfers between devices: 192 us -> 0 us
  blocking collectives: 129 us -> 0 us
  Pallas kernels: 0 us -> 81.4 us
  other arithmetic: 21.5 us -> 0 us
  starting transfers between devices: 20.2 us -> 0 us
  between operations: 17.2 us -> 0.64 us
  matrix products: 12.3 us -> 0 us
  local copies, waits for them, and re-layouts: 6.24 us -> 12.4 us
    unnamed x2 -> x0, waiting for transfers between devices: 183 us -> none
    psum x2 -> x0, blocking collectives: 129 us -> none  [the longest x1 83.1 us: shards(): lax.psum((kernel_part, norm_part, response_part), ('dp', 'rows'))]
    pallas_call x0 -> x1, Pallas kernels: none -> 81.4 us  [shards(): pl.pallas_call(body, out_shape=(jax.ShapeDtypeStruct((R, W, C), BF16), ja...]
    ppermute x4 -> x0, starting transfers between devices: 20.1 us -> none  [the longest x2 17.6 us: with_halo(): before = lax.ppermute(last, axis, up)]
    dot_general x4 -> x0, matrix products: 12.3 us -> none  [the longest x1 4.7 us: shards(): lax.dot_general(preact_grad, normed_in, (((0,), (0,)), ((), ())), preferr...]
    ppermute x4 -> x0, waiting for transfers between devices: 9.11 us -> none  [the longest x2 9.1 us: with_halo(): after = lax.ppermute(leading, axis, down)]
    reduce_sum x7 -> x0, other arithmetic: 8.37 us -> none  [the longest x1 5.15 us: shards(): centered = mixed_flat - jnp.mean(mixed_flat, axis=1, keepdims=True)]
    unnamed x194 -> x5, local copies, waits for them, and re-layouts: 1.18 us -> 7.26 us
  transfers between devices with their start and end apart: 5 -> 0, of which waited for: 2 -> 0; matrix products, arithmetic and copies ran while one was open for 2% -> 0% of each run, Pallas kernels for 0% -> 0%
where the time goes in v1:
time: 94.9 us; the launch traced here: 94.4 us
  Pallas kernels  81.4 us (86%)
  local copies, waits for them, and re-layouts  12.4 us (13%)
    pallas_call x1, Pallas kernels, shards(): pl.pallas_call(body, out_shape=(jax.ShapeDtypeStruct((R, W, C), BF16), ja...  81.4 us
    unnamed x5, local copies, waits for them, and re-layouts  7.26 us

profile of v1, /device:TPU:1, one launch (start us, length us, event | category | flops | bytes accessed | tf_op | source)
XLA Modules:
  0.0 94.4 jit_solution(14838955544448372394)
XLA Ops:
  0.6 1.3 %reshape.25.cb_ref = f32[1,704]{1,0:T(1,128)} reshape(f32[704]{0:T(1024)} %param.17) | data formatting | bytes 5632 | tf_op jit(solution)/shard_map/reshape | solution.py:731
  1.9 1.3 %reshape.26.gain_ref = f32[1,704]{1,0:T(1,128)} reshape(f32[704]{0:T(1024)} %param.18) | data formatting | bytes 5632 | tf_op jit(solution)/shard_map/reshape | solution.py:732
  3.2 1.3 %reshape.27.shift_ref = f32[1,704]{1,0:T(1,128)} reshape(f32[704]{0:T(1024)} %param.19) | data formatting | bytes 5632 | tf_op jit(solution)/shard_map/reshape | solution.py:733
  4.4 1.3 %reshape.28.pb_ref = f32[1,2816]{1,0:T(1,128)} reshape(f32[2816]{0:T(1024)} %param.21) | data formatting | bytes 22528 | tf_op jit(solution)/shard_map/reshape | solution.py:735
  5.7 81.4 %shard_map.155 = (bf16[4,32,704]{2,1,0:T(8,128)(2,1)}, f32[11,704]{1,0:T(8,128)}, f32[7,7,704]{2,1,0:T(8,128)}, f32[2,704]{1,0:T(2,128)}, f32[2,2816]{1,0:T(2,128)}) custom-call(bf16[4,32,704]{2,1,0:T(8,128)(2,1)} %bitcast.15, s32[22,4,32]{2,1,0:T(4,128)} %bitcast.17, bf16[4,32,704]{2,1,0:T(8,128)(2,1)} %bitcast.16, s32[22,4,32]{2,1,0:T(4,128)} %bitcast.18, ...), custom_call_target="tpu_custom_call" | custom-call | tf_op jit(solution)/shard_map/pallas_call | solution.py:710
  87.2 1.6 %copy.22 = bf16[1,4,32,704]{3,2,1,0:T(8,128)(2,1)} copy(bf16[1,4,32,704]{3,2,1,0:T(8,128)(2,1)} %bitcast.14) | data formatting | bytes 360448
  88.8 1.4 %copy.23 = f32[11,704]{1,0:T(8,128)} copy(f32[11,704]{1,0:T(8,128)} %get-tuple-element.21) | data formatting | bytes 61952
  90.2 1.6 %copy.24 = f32[7,7,704]{2,1,0:T(8,128)} copy(f32[7,7,704]{2,1,0:T(8,128)} %get-tuple-element.22) | data formatting | bytes 275968
  91.8 1.3 %copy.25 = f32[2,704]{1,0:T(2,128)} copy(f32[2,704]{1,0:T(2,128)} %get-tuple-element.23) | data formatting | bytes 11264
  93.1 1.3 %copy.26 = f32[2,2816]{1,0:T(2,128)} copy(f32[2,2816]{1,0:T(2,128)} %get-tuple-element.24) | data formatting | bytes 45056

commit v2 on v1

v2 whole, which is shorter than its diff:
```python
import math

import jax
import jax.numpy as jnp
from jax import lax
from jax.experimental import pallas as pl
from jax.experimental.pallas import tpu as pltpu
from jax.sharding import PartitionSpec as P

NORM_EPSILON = 1e-06
RESPONSE_EPSILON = 1e-06
HALF_ROOT = 0.7071067811865476
NORMAL_PEAK = 0.3989422804014327

C = 704
CP = 768
CT = CP // 128
H = 2816
HT = H // 128
R = 4
W = 32
T = R * W
S = H // 8
B = S // 4
U = B // 8
F32 = jnp.float32
BF16 = jnp.bfloat16

ALPHA = (
    0.00022905065861350646,
    0.0034082910107109506,
    0.050955695062380861,
    0.18520832239976145,
    1.128379143519084,
)
BETA = (
    -1.1791602954361697e-7,
    0.000023547966471313185,
    0.0010179625278914885,
    0.014070470171167667,
    0.11098505178285362,
    0.49746925110067538,
    1.0,
)


def erf(v):
    v = jnp.clip(v, -3.7439211627767994, 3.7439211627767994)
    s = v * v
    top = jnp.full_like(s, ALPHA[0])
    for c in ALPHA[1:]:
        top = top * s + c
    low = jnp.full_like(s, BETA[0])
    for c in BETA[1:]:
        low = low * s + c
    return v * top / low


class Phases:
    def __init__(self):
        self.scope = None

    def __call__(self, name=None):
        if self.scope is not None:
            self.scope.__exit__(None, None, None)
        self.scope = jax.named_scope(name) if name else None
        if self.scope is not None:
            self.scope.__enter__()


class Post:
    def __init__(self):
        self.leaving, self.coming, self.inside = [], [], []

    @staticmethod
    def under(cond, f):
        if cond is None:
            f()
        else:
            pl.when(cond)(f)

    def send(self, copy, sends=None, receives=None, came=True):
        self.under(sends, copy.start)
        self.leaving.append((copy, sends))
        if came:
            self.coming.append((copy, receives))
        return copy

    def expect(self, copy, receives):
        self.coming.append((copy, receives))
        return copy

    def arrive(self, copies):
        for copy in copies:
            (entry,) = [e for e in self.coming if e[0] is copy]
            self.coming = [e for e in self.coming if e[0] is not copy]
            self.under(entry[1], copy.wait_recv)

    def left(self, copies):
        for copy in copies:
            (entry,) = [e for e in self.leaving if e[0] is copy]
            self.leaving = [e for e in self.leaving if e[0] is not copy]
            self.under(entry[1], copy.wait_send)

    def move(self, copy, cond=None):
        self.under(cond, copy.start)
        self.inside.append((copy, cond))
        return copy

    def moved(self, copies):
        for copy in copies:
            (entry,) = [e for e in self.inside if e[0] is copy]
            self.inside = [e for e in self.inside if e[0] is not copy]
            self.under(entry[1], copy.wait)

    def drain(self):
        self.moved([e[0] for e in self.inside])
        self.arrive([e[0] for e in self.coming])
        self.left([e[0] for e in self.leaving])


def lanes(i, n=128):
    return pl.ds(pl.multiple_of(i * n, n), n)


def moved(v, d):
    if d == 0:
        return v
    w = lax.broadcasted_iota(jnp.int32, v.shape, 0) + d
    return jnp.where((w >= 0) & (w < W), pltpu.roll(v, (-d) % W, 0), 0.0)


def depthwise(rows, weight):
    out = [None] * R
    for b in range(7):
        for r in range(R):
            acc = rows[r] * weight(0, b)
            for a in range(1, 7):
                acc = acc + rows[r + a] * weight(a, b)
            acc = moved(acc, b - 3)
            out[r] = acc if out[r] is None else out[r] + acc
    return out


def body(
    act_ref, aexp_ref, grad_ref, gexp_ref, ck_ref, cb_ref, gain_ref, shift_ref,
    win_hbm, pb_ref, rg_ref, wout_hbm,
    ig_ref, zr, fin,
    win, wout, ckp, prm, sx, su, xs, up, mg, mx, normed, inv, ni, niall,
    act, gp, dg, pg, pgtf, pgt, pgr, stq, stp, rq, rp, coef, dwf, dwp, dwb, xr, zacc, zs,
    ngb, xf, red, redr, ysum, yr, zsum, zar, og,
    wsem, bsem, ssend, srecv, hsend, hrecv, gsend, grecv, nsend, nrecv, fsend, frecv,
    psend, precv, lsem, xsend, xrecv, zsend, zrecv, rsend, rrecv, ysend, yrecv,
    asend, arecv, tsend, trecv, qsend, qrecv, osend, orecv,
):
    phase = Phases()
    post = Post()
    phase("greet")
    dp, rw = lax.axis_index("dp"), lax.axis_index("rows")
    core = lax.rem(dp, 2)
    y = lax.rem(lax.div(dp, 2), 4)
    zl = lax.div(dp, 8)
    x = lax.div(rw, 2)
    zh = lax.rem(rw, 2)
    z = zh * 4 + zl
    gx = 2 * x + core
    gy = 2 * y + core

    def dev(x=x, y=y, zl=zl, zh=zh, core=core):
        return {"dp": (zl * 4 + y) * 2 + core, "rows": x * 2 + zh}

    def in_gx(i):
        m = lax.rem(gx + i, 8)
        return dev(x=lax.div(m, 2), core=lax.rem(m, 2))

    def in_gy(i):
        m = lax.rem(gy + i, 8)
        return dev(y=lax.div(m, 2), core=lax.rem(m, 2)), m

    def in_z(i):
        m = lax.rem(z + i, 8)
        return dev(zl=lax.rem(m, 4), zh=lax.div(m, 4))

    swap = core != zh
    swap_dev = dev(zh=1 - zh, core=1 - core)
    sib = dev(core=1 - core)

    def remote(src, dst, send, recv, to):
        return pltpu.make_async_remote_copy(
            src_ref=src, dst_ref=dst, send_sem=send, recv_sem=recv,
            device_id=to, device_id_type=pl.DeviceIdType.MESH,
        )

    win_copy = pltpu.make_async_copy(win_hbm, win.at[pl.ds(0, C)], wsem.at[0])
    wout_copy = pltpu.make_async_copy(wout_hbm, wout.at[pl.ds(0, C)], wsem.at[1])
    post.move(win_copy)
    post.move(wout_copy)

    barrier = pltpu.get_barrier_semaphore()

    def greet(d):
        pl.semaphore_signal(
            barrier, inc=1, device_id=d, device_id_type=pl.DeviceIdType.MESH
        )

    @pl.when(swap)
    def _():
        greet(swap_dev)

    for i in range(1, 8):
        greet(in_gx(i))
    for i in range(1, 8):
        d, m = in_gy(i)
        greet(d)
    for i in range(1, 8):
        greet(in_z(i))
    guests = 21 + jnp.where(swap, 1, 0)

    phase("scale")
    member = lax.broadcasted_iota(jnp.int32, (C // 32, CP), 1) // 32
    block = lax.broadcasted_iota(jnp.int32, (C // 32, CP), 0)
    spread = jnp.where(member == block, 1.0, 0.0).astype(BF16)

    def scaled(codes, exps, out):
        for r in range(R):
            power = jnp.exp2(exps[:, r, :].astype(F32)).astype(BF16)
            full = lax.dot_general(
                power, spread, (((0,), (0,)), ((), ())), preferred_element_type=F32
            )
            out[r, :, C - 64 : CP] = jnp.zeros((W, CP - C + 64), BF16)
            out[r, :, 0:C] = (codes[r].astype(F32) * full[:, 0:C]).astype(BF16)

    scaled(act_ref, aexp_ref, sx)

    phase("barrier")
    pl.semaphore_wait(barrier, guests)
    phase("scale2")

    swap_x = remote(sx, xs.at[pl.ds(3, R)], ssend.at[0], srecv.at[0], swap_dev)
    swap_u = remote(su, up, ssend.at[1], srecv.at[1], swap_dev)

    post.send(swap_x, swap, swap)
    scaled(grad_ref, gexp_ref, su)

    @pl.when(jnp.logical_not(swap))
    def _():
        xs[3 : 3 + R] = sx[...]
        up[...] = su[...]

    ckp[...] = jnp.zeros_like(ckp)
    prm[...] = jnp.zeros_like(prm)
    ckp[:, 0:7, 0:C] = ck_ref[...]
    prm[0:1, 0:C] = cb_ref[...].reshape(1, C)
    prm[1:2, 0:C] = gain_ref[...].reshape(1, C)
    prm[2:3, 0:C] = shift_ref[...].reshape(1, C)
    win[C:CP, :] = jnp.zeros((CP - C, H), BF16)
    wout[C:CP, :] = jnp.zeros((CP - C, H), BF16)
    first, last = gx == 0, gx == 7

    @pl.when(first)
    def _():
        xs[0:3] = jnp.zeros((3, W, CP), BF16)
        mg[0:3] = jnp.zeros((3, W, CP), BF16)

    @pl.when(last)
    def _():
        xs[7:10] = jnp.zeros((3, W, CP), BF16)
        mg[7:10] = jnp.zeros((3, W, CP), BF16)

    below, above = lax.rem(gx + 1, 8), lax.rem(gx + 7, 8)
    below_dev = dev(x=lax.div(below, 2), core=lax.rem(below, 2))
    above_dev = dev(x=lax.div(above, 2), core=lax.rem(above, 2))

    def halo(buf, base):
        down = remote(buf.at[pl.ds(4, 3)], buf.at[pl.ds(0, 3)],
                      hsend.at[base], hrecv.at[base], below_dev)
        upward = remote(buf.at[pl.ds(3, 3)], buf.at[pl.ds(7, 3)],
                        hsend.at[base + 1], hrecv.at[base + 1], above_dev)

        post.send(down, jnp.logical_not(last), jnp.logical_not(first))
        post.send(upward, jnp.logical_not(first), jnp.logical_not(last))
        return [down, upward]

    phase("swap_wait")
    post.arrive([swap_x])
    phase("halo_wait")
    x_copies = halo(xs, 0)
    post.send(swap_u, swap, swap)
    post.arrive(x_copies)

    phase("conv")
    def conv_tile(t, _):
        at = lanes(t)
        rows = [xs[i, :, at].astype(F32) for i in range(R + 6)]
        out = depthwise(rows, lambda a, b: ckp[a, b : b + 1, at])
        for r in range(R):
            mx[pl.ds(r * W, W), at] = out[r] + prm[0:1, at]
        return 0

    lax.fori_loop(0, CT, conv_tile, 0)

    phase("norm")
    inside = lax.broadcasted_iota(jnp.int32, (W, CP), 1) < C

    def norm_block(r, _):
        at = pl.ds(pl.multiple_of(r * W, W), W)
        v = mx[at, :]
        centered = jnp.where(inside, v - jnp.sum(v, axis=1, keepdims=True) / C, 0.0)
        var = jnp.sum(centered * centered, axis=1, keepdims=True) / C
        inverse = lax.rsqrt(var + NORM_EPSILON)
        n = centered * inverse
        normed[at, :] = n
        inv[at, :] = jnp.broadcast_to(inverse, (W, 128))
        ni[at, :] = (n * prm[1:2, :] + prm[2:3, :]).astype(BF16)
        return 0

    lax.fori_loop(0, R, norm_block, 0)

    ni_copies = []
    for i in range(1, 4):
        to = dev(y=lax.rem(y + i, 4))
        ni_copies.append(
            remote(ni, niall.at[gy], nsend.at[i - 1], nrecv.at[i - 1], to)
        )
    for c in ni_copies:
        post.send(c)
    niall[gy] = ni[...]

    phase("win_wait")
    stq[...] = jnp.zeros_like(stq)
    stp[...] = jnp.zeros_like(stp)
    red[...] = jnp.zeros_like(red)
    post.moved([win_copy])
    phase("active")

    def active(i, _):
        at = lanes(i, 256)
        bias = [pb_ref[pl.ds(2 * i + k, 1), :] for k in range(2)]
        p = jnp.dot(ni[...], win[:, at], preferred_element_type=F32)
        p = p + jnp.concatenate(bias, axis=1)
        phi = 0.5 * (1.0 + erf(p * HALF_ROOT))
        v = p * phi
        act[:, at] = v
        gp[:, at] = phi + p * (NORMAL_PEAK * jnp.exp(-0.5 * p * p))
        s = jnp.sum(v * v, axis=0, keepdims=True)
        stq[pl.ds(2 * i, 1), :] = s[:, 0:128]
        stq[pl.ds(2 * i + 1, 1), :] = s[:, 128:256]
        return 0

    lax.fori_loop(0, HT // 2, active, 0)

    def to_group(src, dst, send, recv):
        return [
            remote(src, dst.at[gx], send.at[i - 1], recv.at[i - 1], in_gx(i))
            for i in range(1, 8)
        ]

    q_copies = to_group(stq, rq, gsend.at[0], grecv.at[0])
    for c in q_copies:
        post.send(c)
    rq[gx] = stq[...]

    phase("up_wait")
    post.arrive([swap_u])
    post.moved([wout_copy])
    phase("down")
    uf = up[...].reshape(T, CP)

    def downward(i, _):
        at = lanes(i, 256)
        d = jnp.dot(uf, wout[:, at], preferred_element_type=F32)
        dg[:, at] = d
        s = jnp.sum(d * act[:, at], axis=0, keepdims=True)
        stp[pl.ds(2 * i, 1), :] = s[:, 0:128]
        stp[pl.ds(2 * i + 1, 1), :] = s[:, 128:256]
        e = jnp.sum(d, axis=0, keepdims=True)
        red[pl.ds(360 + 2 * i, 1), :] = e[:, 0:128]
        red[pl.ds(361 + 2 * i, 1), :] = e[:, 128:256]
        return 0

    lax.fori_loop(0, HT // 2, downward, 0)
    p_copies = to_group(stp, rp, gsend.at[1], grecv.at[1])
    for c in p_copies:
        post.send(c)
    rp[gx] = stp[...]

    phase("response")
    post.arrive(q_copies)
    squares = rq[0, 0:HT]
    for i in range(1, 8):
        squares = squares + rq[i, 0:HT]
    magnitude = jnp.sqrt(squares + RESPONSE_EPSILON)
    denominator = jnp.sum(magnitude) / H + RESPONSE_EPSILON
    response = magnitude / denominator
    coef[0, 0:HT] = 1.0 + rg_ref[...] * response
    red[336 : 336 + HT] = response * stp[0:HT]
    post.arrive(p_copies)
    products = rp[0, 0:HT]
    for i in range(1, 8):
        products = products + rp[i, 0:HT]
    scaled_products = rg_ref[...] * products
    magnitude_grad = scaled_products / denominator - jnp.sum(
        scaled_products * magnitude
    ) / (denominator * denominator * H)
    coef[1, 0:HT] = magnitude_grad / magnitude

    phase("preact")
    own = pl.ds(pl.multiple_of(gy * 128, 128), 128)
    a_copies = [[], []]
    for h in range(2):

        def preact(i, _):
            j = h * (HT // 2) + i
            at = lanes(j)
            a = coef[0, pl.ds(j, 1), :]
            b = coef[1, pl.ds(j, 1), :]
            g = (dg[:, at] * a + act[:, at] * b) * gp[:, at]
            pg[:, at] = g.astype(BF16)
            turned = g.T
            for k in range(16):
                n = i * 16 + k
                q = lax.div(n, B // 8)
                to = (lax.rem(q, 8) * 2 + lax.div(q, 8)) * B + lax.rem(n, B // 8) * 8
                pgtf[pl.ds(pl.multiple_of(to, 8), 8), :] = turned[8 * k : 8 * k + 8, :]
            return 0

        lax.fori_loop(0, HT // 2, preact, 0)
        pgt[h] = pgtf[...].astype(BF16).reshape(8, S // 2, T)
        for i in range(1, 8):
            to, m = in_gy(i)
            copy = remote(
                pgt.at[h, m], pgr.at[h, :, own], psend.at[h, i - 1], precv.at[h, i - 1], to
            )
            a_copies[h].append(post.send(copy))
        pgr[h, :, own] = pgt[h, gy]

    phase("ni_wait")
    post.arrive(ni_copies)
    f_copies = []
    for k in range(4):
        piece = niall.at[2 * k + core]
        f_copies.append(remote(piece, piece, fsend.at[k], frecv.at[k], sib))
    for c in f_copies:
        post.send(c)

    phase("normed_grad")
    ngb[...] = lax.dot_general(
        pg[...], win[...], (((1,), (1,)), ((), ())), preferred_element_type=F32
    )

    phase("norm_grad")

    def norm_grad(r, sums):
        at = pl.ds(pl.multiple_of(r * W, W), W)
        g = ngb[at, :]
        n = normed[at, :]
        gn = g * n
        s = g * prm[1:2, :]
        m1 = jnp.sum(s, axis=1, keepdims=True) / C
        m2 = jnp.sum(s * n, axis=1, keepdims=True) / C
        v = inv[at, :][:, 0:1] * (s - m1 - n * m2)
        mg[3 + r] = jnp.where(inside, v, 0.0).astype(BF16)
        return (
            sums[0] + jnp.sum(gn, axis=0, keepdims=True),
            sums[1] + jnp.sum(g, axis=0, keepdims=True),
        )

    zero = jnp.zeros((1, CP), F32)
    gain_part, shift_part = lax.fori_loop(0, R, norm_grad, (zero, zero))
    m_copies = halo(mg, 2)

    phase("kernel_grad")
    def kernel_tile(t, _):
        at = lanes(t)
        for i in range(R + 6):
            xf[i] = xs[i, :, at].astype(F32)
        g = [mg[3 + r, :, at].astype(F32) for r in range(R)]
        base = t * 56
        for b in range(7):
            gs = [moved(v, 3 - b) for v in g]
            for a in range(7):
                s = xf[a] * gs[0]
                for r in range(1, R):
                    s = s + xf[a + r] * gs[r]
                red[pl.ds(base + a * 8 + b, 1), :] = jnp.sum(s, axis=0, keepdims=True)
        return 0

    lax.fori_loop(0, CT, kernel_tile, 0)
    for t in range(CT):
        red[56 * t + 7 : 56 * t + 8, :] = gain_part[:, 128 * t : 128 * t + 128]
        red[56 * t + 15 : 56 * t + 16, :] = shift_part[:, 128 * t : 128 * t + 128]

    def share(m):
        return pl.ds(pl.multiple_of(m * 64, 8), 64)

    r_copies = []
    for i in range(1, 8):
        m = lax.rem(gx + i, 8)
        r_copies.append(
            remote(red.at[share(m)], redr.at[gx], rsend.at[i - 1], rrecv.at[i - 1], in_gx(i))
        )
    for c in r_copies:
        post.send(c)
    redr[gx] = red[share(gx), :]

    x_copies = [[], []]

    def weight(h):
        phase("pgr_wait%d" % h)
        post.arrive(a_copies[h])
        if h == 0:
            post.arrive(f_copies)
        phase("dw%d" % h)
        dwf[h, S // 2 :, :] = jnp.zeros((8, CP), F32)
        dwf[h, 0 : S // 2, :] = jnp.dot(
            pgr[h], niall[...].reshape(8 * T, CP), preferred_element_type=F32
        )
        for k in range(4):
            part = jnp.concatenate(
                [dwf[h, B * e + 2 * U * k : B * e + 2 * U * k + 24, :] for e in range(2)]
            )
            dwp[h, k] = part
            dwb[h, k] = part.astype(BF16)
        for i in range(1, 4):
            k = lax.rem(x + i, 4)
            copy = remote(
                dwb.at[h, k], xr.at[h, i - 1], xsend.at[h, i - 1], xrecv.at[h, i - 1], dev(x=k)
            )
            x_copies[h].append(post.send(copy))

    def shares(h):
        phase("x_wait%d" % h)
        post.arrive(x_copies[h])
        phase("z_send%d" % h)
        zacc[h, 48:56, :] = jnp.zeros((8, CP), F32)
        total = dwp[h, x]
        for i in range(3):
            total = total + xr[h, i].astype(F32)
        zacc[h, 0:48, :] = total
        for e in range(2):
            for hi in range(2):
                g = (h * 2 + e) * 2 + hi
                zs[g] = zacc[h, 24 * e + U * hi : 24 * e + U * hi + 16, :].astype(BF16)
                to = hi * 4 + h * 2 + e
                copy = remote(
                    zs.at[g], zr.at[z], zsend.at[g], zrecv.at[z],
                    dev(zl=jnp.int32(h * 2 + e), zh=jnp.int32(hi)),
                )
                post.send(copy, z != to, came=False)

                @pl.when(z == to)
                def _():
                    zr[z] = zs[g]

    weight(0)

    phase("m_wait")
    post.arrive(m_copies)
    phase("back")

    def back_tile(t, _):
        at = lanes(t)
        rows = [mg[i, :, at].astype(F32) for i in range(R + 6)]
        out = depthwise(rows, lambda a, b: ckp[6 - a, 6 - b : 7 - b, at])
        for r in range(R):
            sx[r, :, at] = (out[r] + up[r, :, at].astype(F32)).astype(BF16)
        return 0

    post.left([swap_x])
    lax.fori_loop(0, CT, back_tile, 0)
    og[...] = sx[:, :, 0:C]
    o_copy = remote(og, ig_ref, osend.at[0], orecv.at[0], swap_dev)
    o_local = pltpu.make_async_copy(og, ig_ref, lsem.at[0])
    post.send(o_copy, swap, swap)
    post.move(o_local, jnp.logical_not(swap))

    phase("r_wait")
    post.arrive(r_copies)
    total = redr[0]
    for i in range(1, 8):
        total = total + redr[i]
    ysum[...] = total.reshape(4, 16, 128)
    y_copies = []
    for i in range(1, 4):
        k = lax.rem(y + i, 4)
        copy = remote(ysum.at[k], yr.at[y], ysend.at[i - 1], yrecv.at[i - 1], dev(y=k))
        y_copies.append(post.send(copy))
    yr[y] = ysum[y]

    weight(1)
    phase("y_wait")
    post.arrive(y_copies)
    total = yr[0] + yr[1] + yr[2] + yr[3]
    zsum[...] = total
    s_copies = [
        remote(zsum, zar.at[z], asend.at[i - 1], arecv.at[i - 1], in_z(i))
        for i in range(1, 8)
    ]
    for c in s_copies:
        post.send(c)
    zar[z] = total

    shares(0)
    shares(1)
    z_comes = []
    for k in range(8):
        got = remote(
            zs.at[0], zr.at[k], zsend.at[0], zrecv.at[k],
            dev(zl=jnp.int32(k % 4), zh=jnp.int32(k // 4)),
        )
        z_comes.append(post.expect(got, z != k))

    phase("s_wait")
    post.arrive(s_copies)
    total = zar[0]
    for i in range(1, 8):
        total = total + zar[i]
    mine = pl.ds(pl.multiple_of(gx * 64 + y * 16, 8), 16)
    fin[mine, :] = total
    h_copies = [
        remote(fin.at[mine], fin.at[mine], tsend.at[i - 1], trecv.at[i - 1],
               dev(y=lax.rem(y + i, 4)))
        for i in range(1, 4)
    ]
    for c in h_copies:
        post.send(c)
    phase("h_wait")
    post.arrive(h_copies)
    l_copies = [
        remote(fin.at[share(gx)], fin.at[share(gx)], qsend.at[i - 1], qrecv.at[i - 1], in_gx(i))
        for i in range(1, 8)
    ]
    for c in l_copies:
        post.send(c)
    phase("z_wait")
    post.arrive(z_comes)
    phase("l_wait")
    post.arrive(l_copies)
    phase("o_wait")
    post.arrive([o_copy])
    post.moved([o_local])

    phase("sends")
    post.drain()
    phase()


def finish(ig_ref, zr, fin, out_ref, dw_ref, kg_ref, ng_ref, rp_ref):
    out_ref[...] = ig_ref[...]
    scale = 1.0 / math.sqrt(32.0 * 32.0 * 32.0)
    total = zr[0].astype(F32)
    for k in range(1, 8):
        total = total + zr[k].astype(F32)
    dw_ref[...] = total[0:U, 0:C] * scale
    for t in range(CT):
        a0, n = 128 * t, min(128, C - 128 * t)
        for a in range(7):
            row = 56 * t + 8 * a
            kg_ref[a, :, a0 : a0 + n] = fin[row : row + 7, 0:n] * scale
        ng_ref[0:1, a0 : a0 + n] = fin[56 * t + 7 : 56 * t + 8, 0:n] * scale
        ng_ref[1:2, a0 : a0 + n] = fin[56 * t + 15 : 56 * t + 16, 0:n] * scale
    for i in range(HT):
        rp_ref[0:1, 128 * i : 128 * i + 128] = fin[336 + i : 337 + i, :] * scale
        rp_ref[1:2, 128 * i : 128 * i + 128] = fin[360 + i : 361 + i, :] * scale


def shards(
    act_codes, act_exponents, grad_codes, grad_exponents, conv_kernel, conv_bias,
    norm_gain, norm_shift, proj_in, proj_bias, response_gain, proj_out,
):
    vmem = pl.BlockSpec(memory_space=pltpu.VMEM)
    hbm = pl.BlockSpec(memory_space=pl.ANY)
    dma = pltpu.SemaphoreType.DMA
    scratch = [
        pltpu.VMEM((CP, H), BF16),
        pltpu.VMEM((CP, H), BF16),
        pltpu.VMEM((7, 8, CP), F32),
        pltpu.VMEM((8, CP), F32),
        pltpu.VMEM((R, W, CP), BF16),
        pltpu.VMEM((R, W, CP), BF16),
        pltpu.VMEM((R + 6, W, CP), BF16),
        pltpu.VMEM((R, W, CP), BF16),
        pltpu.VMEM((R + 6, W, CP), BF16),
        pltpu.VMEM((T, CP), F32),
        pltpu.VMEM((T, CP), F32),
        pltpu.VMEM((T, 128), F32),
        pltpu.VMEM((T, CP), BF16),
        pltpu.VMEM((8, T, CP), BF16),
        pltpu.VMEM((T, H), F32),
        pltpu.VMEM((T, H), F32),
        pltpu.VMEM((T, H), F32),
        pltpu.VMEM((T, H), BF16),
        pltpu.VMEM((H // 2, T), F32),
        pltpu.VMEM((2, 8, S // 2, T), BF16),
        pltpu.VMEM((2, S // 2, 8 * T), BF16),
        pltpu.VMEM((24, 128), F32),
        pltpu.VMEM((24, 128), F32),
        pltpu.VMEM((8, 24, 128), F32),
        pltpu.VMEM((8, 24, 128), F32),
        pltpu.VMEM((2, 24, 128), F32),
        pltpu.VMEM((2, S // 2 + 8, CP), F32),
        pltpu.VMEM((2, 4, 48, CP), F32),
        pltpu.VMEM((2, 4, 48, CP), BF16),
        pltpu.VMEM((2, 3, 48, CP), BF16),
        pltpu.VMEM((2, 56, CP), F32),
        pltpu.VMEM((8, 16, CP), BF16),
        pltpu.VMEM((T, CP), F32),
        pltpu.VMEM((R + 6, W, 128), F32),
        pltpu.VMEM((512, 128), F32),
        pltpu.VMEM((8, 64, 128), F32),
        pltpu.VMEM((4, 16, 128), F32),
        pltpu.VMEM((4, 16, 128), F32),
        pltpu.VMEM((16, 128), F32),
        pltpu.VMEM((8, 16, 128), F32),
        pltpu.VMEM((R, W, C), BF16),
        dma((2,)),
        dma((1,)),
        dma((2,)), dma((2,)),
        dma((4,)), dma((4,)),
        dma((2, 7)), dma((2, 7)),
        dma((3,)), dma((3,)),
        dma((4,)), dma((4,)),
        dma((2, 7)), dma((2, 7)),
        dma((1,)),
        dma((2, 3)), dma((2, 3)),
        dma((8,)), dma((8,)),
        dma((7,)), dma((7,)),
        dma((3,)), dma((3,)),
        dma((7,)), dma((7,)),
        dma((3,)), dma((3,)),
        dma((7,)), dma((7,)),
        dma((1,)), dma((1,)),
    ]
    outs = pl.pallas_call(
        body,
        out_shape=(
            jax.ShapeDtypeStruct((R, W, C), BF16),
            jax.ShapeDtypeStruct((8, 16, CP), BF16),
            jax.ShapeDtypeStruct((512, 128), F32),
        ),
        in_specs=[vmem] * 8 + [hbm, vmem, vmem, hbm],
        out_specs=(hbm, vmem, vmem),
        scratch_shapes=scratch,
        compiler_params=pltpu.CompilerParams(
            collective_id=0, has_side_effects=True, vmem_limit_bytes=56 * 1024 * 1024
        ),
    )(
        act_codes[0],
        act_exponents[0].transpose(2, 0, 1),
        grad_codes[0],
        grad_exponents[0].transpose(2, 0, 1),
        conv_kernel,
        conv_bias,
        norm_gain,
        norm_shift,
        proj_in.T,
        proj_bias.reshape(HT, 128),
        response_gain.reshape(HT, 128),
        proj_out.T,
    )
    results = pl.pallas_call(
        finish,
        out_shape=(
            jax.ShapeDtypeStruct((R, W, C), BF16),
            jax.ShapeDtypeStruct((U, C), F32),
            jax.ShapeDtypeStruct((7, 7, C), F32),
            jax.ShapeDtypeStruct((2, C), F32),
            jax.ShapeDtypeStruct((2, H), F32),
        ),
        in_specs=[vmem] * 3,
        out_specs=(vmem,) * 5,
    )(*outs)
    return (results[0][None],) + tuple(results[1:])


def solution(mesh):
    strips = P("dp", "rows", None, None)
    return jax.shard_map(
        shards,
        mesh=mesh,
        in_specs=(strips,) * 4 + (P(),) * 8,
        out_specs=(strips, P(("dp", "rows"), None), P(), P(), P()),
        check_vma=False,
    )
```

time: 94.9 us -> 71.2 us (0.75)
  local copies, waits for them, and re-layouts: 12.4 us -> 0 us
  Pallas kernels: 81.4 us -> 70.4 us
    pallas_call x1, Pallas kernels: 81.4 us -> 68.4 us  [shards(): pl.pallas_call(body, out_shape=(jax.ShapeDtypeStruct((R, W, C), BF16), ja...]
    unnamed x5 -> x0, local copies, waits for them, and re-layouts: 7.26 us -> none
    reshape x4 -> x0, local copies, waits for them, and re-layouts: 5.11 us -> none  [the longest x1 1.31 us: shards(): proj_bias.reshape(1, H)]
    pallas_call x0 -> x1, Pallas kernels: none -> 1.98 us  [shards(): pl.pallas_call(finish, out_shape=(jax.ShapeDtypeStruct((R, W, C), BF16),...]
where the time goes in v2:
time: 71.2 us; the launch traced here: 71 us
  Pallas kernels  70.4 us (99%)
    pallas_call x1, Pallas kernels, shards(): pl.pallas_call(body, out_shape=(jax.ShapeDtypeStruct((R, W, C), BF16), ja...  68.4 us
    pallas_call x1, Pallas kernels, shards(): pl.pallas_call(finish, out_shape=(jax.ShapeDtypeStruct((R, W, C), BF16),...  1.98 us

profile of v2, /device:TPU:1, one launch (start us, length us, event | category | flops | bytes accessed | tf_op | source)
XLA Modules:
  0.0 71.0 jit_solution(16129972542615127221)
XLA Ops:
  0.6 68.4 %shard_map.155 = (bf16[4,32,704]{2,1,0:T(8,128)(2,1)}, bf16[8,16,768]{2,1,0:T(8,128)(2,1)}, f32[512,128]{1,0:T(8,128)}) custom-call(bf16[4,32,704]{2,1,0:T(8,128)(2,1)} %bitcast.15, s32[22,4,32]{2,1,0:T(4,128)} %bitcast.17, bf16[4,32,704]{2,1,0:T(8,128)(2,1)} %bitcast.16, s32[22,4,32]{2,1,0:T(4,128)} %bitcast.18, f32[7,7,704]{2,1,0:T(8,128)} %ck_ref.1, ...), custom_call_target="tpu_custom_call" | custom-call | tf_op jit(solution)/shard_map/pallas_call | solution.py:734
  69.1 2.0 %shard_map.156 = (bf16[4,32,704]{2,1,0:T(8,128)(2,1)}, f32[11,704]{1,0:T(8,128)}, f32[7,7,704]{2,1,0:T(8,128)}, f32[2,704]{1,0:T(2,128)}, f32[2,2816]{1,0:T(2,128)}) custom-call(bf16[4,32,704]{2,1,0:T(8,128)(2,1)} %get-tuple-element.13.ig_ref, bf16[8,16,768]{2,1,0:T(8,128)(2,1)} %get-tuple-element.14.zr, f32[512,128]{1,0:T(8,128)} %get-tuple-element.15.fin), custom_call_target="tpu_custom_call" | custom-call | tf_op jit(solution)/shard_map/pallas_call | solution.py:761

commit v3 on v2

--- a/solution.py
+++ b/solution.py
@@ -86,9 +86,14 @@
             self.coming.append((copy, receives))
         return copy
 
-    def expect(self, copy, receives):
-        self.coming.append((copy, receives))
-        return copy
+    def together(self, copies, whole, sends=None):
+        sends = sends or [None] * len(copies)
+        for copy, cond in zip(copies, sends, strict=True):
+            self.under(cond, copy.start)
+        if whole is not None:
+            self.leaving.append((whole, None))
+            self.coming.append((whole, None))
+        return [whole]
 
     def arrive(self, copies):
         for copy in copies:
@@ -143,15 +148,16 @@
 
 
 def body(
-    act_ref, aexp_ref, grad_ref, gexp_ref, ck_ref, cb_ref, gain_ref, shift_ref,
-    win_hbm, pb_ref, rg_ref, wout_hbm,
+    act_in, aexp_in, grad_in, gexp_in, ck_in, cb_in, gain_in, shift_in,
+    win_hbm, pb_in, rg_in, wout_hbm,
     ig_ref, zr, fin,
+    act_ref, aexp_ref, grad_ref, gexp_ref, ck_ref, cb_ref, gain_ref, shift_ref, pb_ref, rg_ref,
     win, wout, ckp, prm, sx, su, xs, up, mg, mx, normed, inv, ni, niall,
     act, gp, dg, pg, pgtf, pgt, pgr, stq, stp, rq, rp, coef, dwf, dwp, dwb, xr, zacc, zs,
-    ngb, xf, red, redr, ysum, yr, zsum, zar, og,
-    wsem, bsem, ssend, srecv, hsend, hrecv, gsend, grecv, nsend, nrecv, fsend, frecv,
-    psend, precv, lsem, xsend, xrecv, zsend, zrecv, rsend, rrecv, ysend, yrecv,
-    asend, arecv, tsend, trecv, qsend, qrecv, osend, orecv,
+    ngb, xf, red, redr, zsum, zar, back, og,
+    wsem, isem, ssend, srecv, hsend, hrecv, gsend, grecv, nsend, nrecv, fsend, frecv,
+    psend, precv, lsem, xsend, xrecv, zsend, zrecv, rsend, rrecv,
+    zlocal, asend, arecv, qsend, qrecv, osend, orecv,
 ):
     phase = Phases()
     post = Post()
@@ -177,6 +183,12 @@
         m = lax.rem(gy + i, 8)
         return dev(y=lax.div(m, 2), core=lax.rem(m, 2)), m
 
+    def in_layer(iy, i):
+        m, yy = lax.rem(gx + i, 8), lax.rem(y + iy, 4)
+        return dev(x=lax.div(m, 2), core=lax.rem(m, 2), y=yy), m, yy
+
+    layer = [(iy, i) for iy in range(4) for i in range(8)][1:]
+
     def in_z(i):
         m = lax.rem(z + i, 8)
         return dev(zl=lax.rem(m, 4), zh=lax.div(m, 4))
@@ -191,10 +203,18 @@
             device_id=to, device_id_type=pl.DeviceIdType.MESH,
         )
 
+    loads = [
+        pltpu.make_async_copy(a, b, isem.at[k])
+        for k, (a, b) in enumerate(
+            (
+                (aexp_in, aexp_ref), (act_in, act_ref), (gexp_in, gexp_ref), (grad_in, grad_ref),
+                (ck_in, ck_ref), (cb_in, cb_ref), (gain_in, gain_ref), (shift_in, shift_ref),
+                (pb_in, pb_ref), (rg_in, rg_ref),
+            )
+        )
+    ]
     win_copy = pltpu.make_async_copy(win_hbm, win.at[pl.ds(0, C)], wsem.at[0])
     wout_copy = pltpu.make_async_copy(wout_hbm, wout.at[pl.ds(0, C)], wsem.at[1])
-    post.move(win_copy)
-    post.move(wout_copy)
 
     barrier = pltpu.get_barrier_semaphore()
 
@@ -207,15 +227,14 @@
     def _():
         greet(swap_dev)
 
-    for i in range(1, 8):
-        greet(in_gx(i))
-    for i in range(1, 8):
-        d, m = in_gy(i)
-        greet(d)
+    for iy, i in layer:
+        greet(in_layer(iy, i)[0])
     for i in range(1, 8):
         greet(in_z(i))
-    guests = 21 + jnp.where(swap, 1, 0)
-
+    guests = 38 + jnp.where(swap, 1, 0)
+
+    for c in loads + [win_copy, wout_copy]:
+        post.move(c)
     phase("scale")
     member = lax.broadcasted_iota(jnp.int32, (C // 32, CP), 1) // 32
     block = lax.broadcasted_iota(jnp.int32, (C // 32, CP), 0)
@@ -230,16 +249,22 @@
             out[r, :, C - 64 : CP] = jnp.zeros((W, CP - C + 64), BF16)
             out[r, :, 0:C] = (codes[r].astype(F32) * full[:, 0:C]).astype(BF16)
 
+    post.moved(loads[0:2])
     scaled(act_ref, aexp_ref, sx)
 
     phase("barrier")
     pl.semaphore_wait(barrier, guests)
     phase("scale2")
 
-    swap_x = remote(sx, xs.at[pl.ds(3, R)], ssend.at[0], srecv.at[0], swap_dev)
-    swap_u = remote(su, up, ssend.at[1], srecv.at[1], swap_dev)
-
-    post.send(swap_x, swap, swap)
+    thirds = [pl.ds(CP // 3 * k, CP // 3) for k in range(3)]
+    swap_x = [
+        remote(sx.at[:, :, at], xs.at[pl.ds(3, R), :, at], ssend.at[k], srecv.at[k], swap_dev)
+        for k, at in enumerate(thirds)
+    ]
+    swap_u = remote(su, up, ssend.at[3], srecv.at[3], swap_dev)
+
+    post.send(swap_x[0], swap, swap)
+    post.moved(loads[2:])
     scaled(grad_ref, gexp_ref, su)
 
     @pl.when(jnp.logical_not(swap))
@@ -271,24 +296,16 @@
     below_dev = dev(x=lax.div(below, 2), core=lax.rem(below, 2))
     above_dev = dev(x=lax.div(above, 2), core=lax.rem(above, 2))
 
-    def halo(buf, base):
-        down = remote(buf.at[pl.ds(4, 3)], buf.at[pl.ds(0, 3)],
+    def halo(buf, base, at=slice(None)):
+        down = remote(buf.at[pl.ds(4, 3), :, at], buf.at[pl.ds(0, 3), :, at],
                       hsend.at[base], hrecv.at[base], below_dev)
-        upward = remote(buf.at[pl.ds(3, 3)], buf.at[pl.ds(7, 3)],
+        upward = remote(buf.at[pl.ds(3, 3), :, at], buf.at[pl.ds(7, 3), :, at],
                         hsend.at[base + 1], hrecv.at[base + 1], above_dev)
 
         post.send(down, jnp.logical_not(last), jnp.logical_not(first))
         post.send(upward, jnp.logical_not(first), jnp.logical_not(last))
         return [down, upward]
 
-    phase("swap_wait")
-    post.arrive([swap_x])
-    phase("halo_wait")
-    x_copies = halo(xs, 0)
-    post.send(swap_u, swap, swap)
-    post.arrive(x_copies)
-
-    phase("conv")
     def conv_tile(t, _):
         at = lanes(t)
         rows = [xs[i, :, at].astype(F32) for i in range(R + 6)]
@@ -297,8 +314,22 @@
             mx[pl.ds(r * W, W), at] = out[r] + prm[0:1, at]
         return 0
 
-    lax.fori_loop(0, CT, conv_tile, 0)
-
+    near = []
+    for k in range(4):
+        if k < 3:
+            phase("swap_wait%d" % k)
+            post.left([swap_x[k]])
+            if k < 2:
+                post.send(swap_x[k + 1], swap, swap)
+            else:
+                post.send(swap_u, swap, swap)
+            post.arrive([swap_x[k]])
+            near.append(halo(xs, 2 * k, thirds[k]))
+        if k > 0:
+            phase("halo_wait%d" % (k - 1))
+            post.arrive(near[k - 1])
+            phase("conv%d" % (k - 1))
+            lax.fori_loop((k - 1) * CT // 3, k * CT // 3, conv_tile, 0)
     phase("norm")
     inside = lax.broadcasted_iota(jnp.int32, (W, CP), 1) < C
 
@@ -316,14 +347,14 @@
 
     lax.fori_loop(0, R, norm_block, 0)
 
-    ni_copies = []
-    for i in range(1, 4):
-        to = dev(y=lax.rem(y + i, 4))
-        ni_copies.append(
-            remote(ni, niall.at[gy], nsend.at[i - 1], nrecv.at[i - 1], to)
-        )
-    for c in ni_copies:
-        post.send(c)
+    three = niall.at[pl.ds(0, 3)]
+    ni_copies = post.together(
+        [
+            remote(ni, niall.at[gy], nsend, nrecv, dev(y=lax.rem(y + i, 4)))
+            for i in range(1, 4)
+        ],
+        remote(three, three, nsend, nrecv, sib),
+    )
     niall[gy] = ni[...]
 
     phase("win_wait")
@@ -347,17 +378,16 @@
         stq[pl.ds(2 * i + 1, 1), :] = s[:, 128:256]
         return 0
 
-    lax.fori_loop(0, HT // 2, active, 0)
+    lax.fori_loop(0, HT // 2, active, 0, unroll=True)
 
     def to_group(src, dst, send, recv):
-        return [
-            remote(src, dst.at[gx], send.at[i - 1], recv.at[i - 1], in_gx(i))
-            for i in range(1, 8)
-        ]
+        seven = dst.at[pl.ds(0, 7)]
+        return post.together(
+            [remote(src, dst.at[gx], send, recv, in_gx(i)) for i in range(1, 8)],
+            remote(seven, seven, send, recv, sib),
+        )
 
     q_copies = to_group(stq, rq, gsend.at[0], grecv.at[0])
-    for c in q_copies:
-        post.send(c)
     rq[gx] = stq[...]
 
     phase("up_wait")
@@ -366,10 +396,11 @@
     phase("down")
     uf = up[...].reshape(T, CP)
 
+    dg[...] = jnp.dot(uf, wout[...], preferred_element_type=F32)
+
     def downward(i, _):
         at = lanes(i, 256)
-        d = jnp.dot(uf, wout[:, at], preferred_element_type=F32)
-        dg[:, at] = d
+        d = dg[:, at]
         s = jnp.sum(d * act[:, at], axis=0, keepdims=True)
         stp[pl.ds(2 * i, 1), :] = s[:, 0:128]
         stp[pl.ds(2 * i + 1, 1), :] = s[:, 128:256]
@@ -378,10 +409,8 @@
         red[pl.ds(361 + 2 * i, 1), :] = e[:, 128:256]
         return 0
 
-    lax.fori_loop(0, HT // 2, downward, 0)
+    lax.fori_loop(0, HT // 2, downward, 0, unroll=True)
     p_copies = to_group(stp, rp, gsend.at[1], grecv.at[1])
-    for c in p_copies:
-        post.send(c)
     rp[gx] = stp[...]
 
     phase("response")
@@ -424,28 +453,32 @@
                 pgtf[pl.ds(pl.multiple_of(to, 8), 8), :] = turned[8 * k : 8 * k + 8, :]
             return 0
 
-        lax.fori_loop(0, HT // 2, preact, 0)
+        lax.fori_loop(0, HT // 2, preact, 0, unroll=True)
         pgt[h] = pgtf[...].astype(BF16).reshape(8, S // 2, T)
+        copies = []
         for i in range(1, 8):
             to, m = in_gy(i)
-            copy = remote(
-                pgt.at[h, m], pgr.at[h, :, own], psend.at[h, i - 1], precv.at[h, i - 1], to
+            copies.append(
+                remote(pgt.at[h, m], pgr.at[h, :, own], psend.at[h], precv.at[h], to)
             )
-            a_copies[h].append(post.send(copy))
+        seven = pgt.at[h, pl.ds(0, 7)]
+        a_copies[h] = post.together(
+            copies, remote(seven, seven, psend.at[h], precv.at[h], sib)
+        )
         pgr[h, :, own] = pgt[h, gy]
-
-    phase("ni_wait")
-    post.arrive(ni_copies)
-    f_copies = []
-    for k in range(4):
-        piece = niall.at[2 * k + core]
-        f_copies.append(remote(piece, piece, fsend.at[k], frecv.at[k], sib))
-    for c in f_copies:
-        post.send(c)
 
     phase("normed_grad")
     ngb[...] = lax.dot_general(
         pg[...], win[...], (((1,), (1,)), ((), ())), preferred_element_type=F32
+    )
+
+    phase("ni_wait")
+    post.arrive(ni_copies)
+    pieces = [niall.at[2 * k + core] for k in range(4)]
+    four = niall.at[pl.ds(0, 4)]
+    f_copies = post.together(
+        [remote(p, p, fsend, frecv, sib) for p in pieces],
+        remote(four, four, fsend, frecv, sib),
     )
 
     phase("norm_grad")
@@ -467,7 +500,7 @@
 
     zero = jnp.zeros((1, CP), F32)
     gain_part, shift_part = lax.fori_loop(0, R, norm_grad, (zero, zero))
-    m_copies = halo(mg, 2)
+    m_copies = halo(mg, 6)
 
     phase("kernel_grad")
     def kernel_tile(t, _):
@@ -490,18 +523,18 @@
         red[56 * t + 7 : 56 * t + 8, :] = gain_part[:, 128 * t : 128 * t + 128]
         red[56 * t + 15 : 56 * t + 16, :] = shift_part[:, 128 * t : 128 * t + 128]
 
-    def share(m):
-        return pl.ds(pl.multiple_of(m * 64, 8), 64)
-
-    r_copies = []
-    for i in range(1, 8):
-        m = lax.rem(gx + i, 8)
-        r_copies.append(
-            remote(red.at[share(m)], redr.at[gx], rsend.at[i - 1], rrecv.at[i - 1], in_gx(i))
-        )
-    for c in r_copies:
-        post.send(c)
-    redr[gx] = red[share(gx), :]
+    def piece(m, yy):
+        return pl.ds(pl.multiple_of(m * 64 + yy * 16, 8), 16)
+
+    mine = piece(gx, y)
+    place = gx * 4 + y
+    copies = []
+    for iy, i in layer:
+        to, m, yy = in_layer(iy, i)
+        copies.append(remote(red.at[piece(m, yy)], redr.at[place], rsend, rrecv, to))
+    most = redr.at[pl.ds(0, 31)]
+    r_copies = post.together(copies, remote(most, most, rsend, rrecv, sib))
+    redr[place] = red[mine, :]
 
     x_copies = [[], []]
 
@@ -521,12 +554,15 @@
             )
             dwp[h, k] = part
             dwb[h, k] = part.astype(BF16)
+        copies = []
         for i in range(1, 4):
             k = lax.rem(x + i, 4)
-            copy = remote(
-                dwb.at[h, k], xr.at[h, i - 1], xsend.at[h, i - 1], xrecv.at[h, i - 1], dev(x=k)
+            copies.append(
+                remote(dwb.at[h, k], xr.at[h, i - 1], xsend.at[h], xrecv.at[h], dev(x=k))
             )
-            x_copies[h].append(post.send(copy))
+        x_copies[h] = post.together(
+            copies, remote(xr.at[h], xr.at[h], xsend.at[h], xrecv.at[h], sib)
+        )
 
     def shares(h):
         phase("x_wait%d" % h)
@@ -543,14 +579,12 @@
                 zs[g] = zacc[h, 24 * e + U * hi : 24 * e + U * hi + 16, :].astype(BF16)
                 to = hi * 4 + h * 2 + e
                 copy = remote(
-                    zs.at[g], zr.at[z], zsend.at[g], zrecv.at[z],
+                    zs.at[g], zr.at[z], zsend, zrecv,
                     dev(zl=jnp.int32(h * 2 + e), zh=jnp.int32(hi)),
                 )
-                post.send(copy, z != to, came=False)
-
-                @pl.when(z == to)
-                def _():
-                    zr[z] = zs[g]
+                post.together([copy], None, [z != to])
+                own_share = pltpu.make_async_copy(zs.at[g], zr.at[z], zlocal)
+                pl.when(z == to)(own_share.start)
 
     weight(0)
 
@@ -566,79 +600,55 @@
             sx[r, :, at] = (out[r] + up[r, :, at].astype(F32)).astype(BF16)
         return 0
 
-    post.left([swap_x])
     lax.fori_loop(0, CT, back_tile, 0)
     og[...] = sx[:, :, 0:C]
     o_copy = remote(og, ig_ref, osend.at[0], orecv.at[0], swap_dev)
     o_local = pltpu.make_async_copy(og, ig_ref, lsem.at[0])
+
     post.send(o_copy, swap, swap)
     post.move(o_local, jnp.logical_not(swap))
+    weight(1)
 
     phase("r_wait")
     post.arrive(r_copies)
     total = redr[0]
-    for i in range(1, 8):
+    for i in range(1, 32):
         total = total + redr[i]
-    ysum[...] = total.reshape(4, 16, 128)
-    y_copies = []
-    for i in range(1, 4):
-        k = lax.rem(y + i, 4)
-        copy = remote(ysum.at[k], yr.at[y], ysend.at[i - 1], yrecv.at[i - 1], dev(y=k))
-        y_copies.append(post.send(copy))
-    yr[y] = ysum[y]
-
-    weight(1)
-    phase("y_wait")
-    post.arrive(y_copies)
-    total = yr[0] + yr[1] + yr[2] + yr[3]
     zsum[...] = total
-    s_copies = [
-        remote(zsum, zar.at[z], asend.at[i - 1], arecv.at[i - 1], in_z(i))
-        for i in range(1, 8)
-    ]
-    for c in s_copies:
-        post.send(c)
+    seven = zar.at[pl.ds(0, 7)]
+    s_copies = post.together(
+        [remote(zsum, zar.at[z], asend, arecv, in_z(i)) for i in range(1, 8)],
+        remote(seven, seven, asend, arecv, sib),
+    )
     zar[z] = total
 
     shares(0)
-    shares(1)
-    z_comes = []
-    for k in range(8):
-        got = remote(
-            zs.at[0], zr.at[k], zsend.at[0], zrecv.at[k],
-            dev(zl=jnp.int32(k % 4), zh=jnp.int32(k // 4)),
-        )
-        z_comes.append(post.expect(got, z != k))
 
     phase("s_wait")
     post.arrive(s_copies)
     total = zar[0]
     for i in range(1, 8):
         total = total + zar[i]
-    mine = pl.ds(pl.multiple_of(gx * 64 + y * 16, 8), 16)
-    fin[mine, :] = total
-    h_copies = [
-        remote(fin.at[mine], fin.at[mine], tsend.at[i - 1], trecv.at[i - 1],
-               dev(y=lax.rem(y + i, 4)))
-        for i in range(1, 4)
-    ]
-    for c in h_copies:
-        post.send(c)
-    phase("h_wait")
-    post.arrive(h_copies)
-    l_copies = [
-        remote(fin.at[share(gx)], fin.at[share(gx)], qsend.at[i - 1], qrecv.at[i - 1], in_gx(i))
-        for i in range(1, 8)
-    ]
-    for c in l_copies:
-        post.send(c)
+    back[...] = total
+    l_copies = post.together(
+        [
+            remote(back, fin.at[mine], qsend, qrecv, in_layer(iy, i)[0])
+            for iy, i in layer
+        ],
+        remote(most, most, qsend, qrecv, sib),
+    )
+    own_sums = post.move(pltpu.make_async_copy(back, fin.at[mine], lsem.at[1]))
+    shares(1)
+    seven = zs.at[pl.ds(0, 7)]
+    z_comes = post.together([], remote(seven, seven, zsend, zrecv, sib))
     phase("z_wait")
     post.arrive(z_comes)
     phase("l_wait")
     post.arrive(l_copies)
     phase("o_wait")
     post.arrive([o_copy])
-    post.moved([o_local])
+    post.moved([o_local, own_sums])
+    pltpu.make_async_copy(zs.at[0], zr.at[z], zlocal).wait()
 
     phase("sends")
     post.drain()
@@ -672,6 +682,16 @@
     hbm = pl.BlockSpec(memory_space=pl.ANY)
     dma = pltpu.SemaphoreType.DMA
     scratch = [
+        pltpu.VMEM((R, W, C), BF16),
+        pltpu.VMEM((C // 32, R, W), jnp.int32),
+        pltpu.VMEM((R, W, C), BF16),
+        pltpu.VMEM((C // 32, R, W), jnp.int32),
+        pltpu.VMEM((7, 7, C), F32),
+        pltpu.VMEM((C,), F32),
+        pltpu.VMEM((C,), F32),
+        pltpu.VMEM((C,), F32),
+        pltpu.VMEM((HT, 128), F32),
+        pltpu.VMEM((HT, 128), F32),
         pltpu.VMEM((CP, H), BF16),
         pltpu.VMEM((CP, H), BF16),
         pltpu.VMEM((7, 8, CP), F32),
@@ -707,28 +727,25 @@
         pltpu.VMEM((T, CP), F32),
         pltpu.VMEM((R + 6, W, 128), F32),
         pltpu.VMEM((512, 128), F32),
-        pltpu.VMEM((8, 64, 128), F32),
-        pltpu.VMEM((4, 16, 128), F32),
-        pltpu.VMEM((4, 16, 128), F32),
+        pltpu.VMEM((32, 16, 128), F32),
         pltpu.VMEM((16, 128), F32),
         pltpu.VMEM((8, 16, 128), F32),
+        pltpu.VMEM((16, 128), F32),
         pltpu.VMEM((R, W, C), BF16),
+        dma((2,)), dma((10,)),
+        dma((4,)), dma((4,)),
+        dma((8,)), dma((8,)),
+        dma((2,)), dma((2,)),
+        dma, dma,
+        dma, dma,
+        dma((2,)), dma((2,)),
         dma((2,)),
-        dma((1,)),
         dma((2,)), dma((2,)),
-        dma((4,)), dma((4,)),
-        dma((2, 7)), dma((2, 7)),
-        dma((3,)), dma((3,)),
-        dma((4,)), dma((4,)),
-        dma((2, 7)), dma((2, 7)),
-        dma((1,)),
-        dma((2, 3)), dma((2, 3)),
-        dma((8,)), dma((8,)),
-        dma((7,)), dma((7,)),
-        dma((3,)), dma((3,)),
-        dma((7,)), dma((7,)),
-        dma((3,)), dma((3,)),
-        dma((7,)), dma((7,)),
+        dma, dma,
+        dma, dma,
+        dma,
+        dma, dma,
+        dma, dma,
         dma((1,)), dma((1,)),
     ]
     outs = pl.pallas_call(
@@ -738,8 +755,8 @@
             jax.ShapeDtypeStruct((8, 16, CP), BF16),
             jax.ShapeDtypeStruct((512, 128), F32),
         ),
-        in_specs=[vmem] * 8 + [hbm, vmem, vmem, hbm],
-        out_specs=(hbm, vmem, vmem),
+        in_specs=[hbm] * 12,
+        out_specs=(hbm,) * 3,
         scratch_shapes=scratch,
         compiler_params=pltpu.CompilerParams(
             collective_id=0, has_side_effects=True, vmem_limit_bytes=56 * 1024 * 1024

time: 71.2 us -> 62 us (0.87)
  Pallas kernels: 70.4 us -> 61.2 us
    pallas_call x1, Pallas kernels: 68.4 us -> 59.2 us  [shards(): pl.pallas_call(body, out_shape=(jax.ShapeDtypeStruct((R, W, C), BF16), ja...]
where the time goes in v3:
time: 62 us; the launch traced here: 61.9 us
  Pallas kernels  61.2 us (99%)
  between operations  0.64 us (1%)
    pallas_call x1, Pallas kernels, shards(): pl.pallas_call(body, out_shape=(jax.ShapeDtypeStruct((R, W, C), BF16), ja...  59.2 us
    pallas_call x1, Pallas kernels, shards(): pl.pallas_call(finish, out_shape=(jax.ShapeDtypeStruct((R, W, C), BF16),...  1.98 us

profile of v3, /device:TPU:1, one launch (start us, length us, event | category | flops | bytes accessed | tf_op | source)
XLA Modules:
  0.0 61.9 jit_solution(5429153689688286066)
XLA Ops:
  0.6 59.2 %shard_map.155 = (bf16[4,32,704]{2,1,0:T(8,128)(2,1)}, bf16[8,16,768]{2,1,0:T(8,128)(2,1)}, f32[512,128]{1,0:T(8,128)}) custom-call(bf16[4,32,704]{2,1,0:T(8,128)(2,1)} %bitcast.15, s32[22,4,32]{2,1,0:T(4,128)} %bitcast.17, bf16[4,32,704]{2,1,0:T(8,128)(2,1)} %bitcast.16, s32[22,4,32]{2,1,0:T(4,128)} %bitcast.18, f32[7,7,704]{2,1,0:T(8,128)} %ck_in.1, ...), custom_call_target="tpu_custom_call" | custom-call | tf_op jit(solution)/shard_map/pallas_call | solution.py:751
  59.9 2.0 %shard_map.156 = (bf16[4,32,704]{2,1,0:T(8,128)(2,1)}, f32[11,704]{1,0:T(8,128)}, f32[7,7,704]{2,1,0:T(8,128)}, f32[2,704]{1,0:T(2,128)}, f32[2,2816]{1,0:T(2,128)}) custom-call(bf16[4,32,704]{2,1,0:T(8,128)(2,1)} %get-tuple-element.13.ig_ref, bf16[8,16,768]{2,1,0:T(8,128)(2,1)} %get-tuple-element.14.zr, f32[512,128]{1,0:T(8,128)} %get-tuple-element.15.fin), custom_call_target="tpu_custom_call" | custom-call | tf_op jit(solution)/shard_map/pallas_call | solution.py:778

commit v4 on v3

--- a/solution.py
+++ b/solution.py
@@ -95,6 +95,11 @@
             self.coming.append((whole, None))
         return [whole]
 
+    def partly(self, leaving, coming):
+        self.leaving += leaving
+        self.coming += coming
+        return [whole for whole, _ in coming]
+
     def arrive(self, copies):
         for copy in copies:
             (entry,) = [e for e in self.coming if e[0] is copy]
@@ -154,9 +159,9 @@
     act_ref, aexp_ref, grad_ref, gexp_ref, ck_ref, cb_ref, gain_ref, shift_ref, pb_ref, rg_ref,
     win, wout, ckp, prm, sx, su, xs, up, mg, mx, normed, inv, ni, niall,
     act, gp, dg, pg, pgtf, pgt, pgr, stq, stp, rq, rp, coef, dwf, dwp, dwb, xr, zacc, zs,
-    ngb, xf, red, redr, zsum, zar, back, og,
+    ngb, xf, red, redr, ysum, yr, zsum, zar, back, og,
     wsem, isem, ssend, srecv, hsend, hrecv, gsend, grecv, nsend, nrecv, fsend, frecv,
-    psend, precv, lsem, xsend, xrecv, zsend, zrecv, rsend, rrecv,
+    psend, precv, lsem, xsend, xrecv, zsend, zrecv, rsend, rrecv, ysend, yrecv,
     zlocal, asend, arecv, qsend, qrecv, osend, orecv,
 ):
     phase = Phases()
@@ -216,6 +221,9 @@
     win_copy = pltpu.make_async_copy(win_hbm, win.at[pl.ds(0, C)], wsem.at[0])
     wout_copy = pltpu.make_async_copy(wout_hbm, wout.at[pl.ds(0, C)], wsem.at[1])
 
+    for c in loads + [win_copy, wout_copy]:
+        post.move(c)
+
     barrier = pltpu.get_barrier_semaphore()
 
     def greet(d):
@@ -233,8 +241,6 @@
         greet(in_z(i))
     guests = 38 + jnp.where(swap, 1, 0)
 
-    for c in loads + [win_copy, wout_copy]:
-        post.move(c)
     phase("scale")
     member = lax.broadcasted_iota(jnp.int32, (C // 32, CP), 1) // 32
     block = lax.broadcasted_iota(jnp.int32, (C // 32, CP), 0)
@@ -436,6 +442,25 @@
     phase("preact")
     own = pl.ds(pl.multiple_of(gy * 128, 128), 128)
     a_copies = [[], []]
+
+    def exchange(h):
+        copies = []
+        for i in range(1, 8):
+            to, m = in_gy(i)
+            copies.append(
+                remote(pgt.at[h, m], pgr.at[h, :, own], psend.at[h], precv.at[h], to)
+            )
+        seven = pgt.at[h, pl.ds(0, 7)]
+        a_copies[h] = post.together(
+            copies, remote(seven, seven, psend.at[h], precv.at[h], sib)
+        )
+
+    def backward(h):
+        at = pl.ds(h * (H // 2), H // 2)
+        return lax.dot_general(
+            pg[:, at], win[:, at], (((1,), (1,)), ((), ())), preferred_element_type=F32
+        )
+
     for h in range(2):
 
         def preact(i, _):
@@ -455,32 +480,14 @@
 
         lax.fori_loop(0, HT // 2, preact, 0, unroll=True)
         pgt[h] = pgtf[...].astype(BF16).reshape(8, S // 2, T)
-        copies = []
-        for i in range(1, 8):
-            to, m = in_gy(i)
-            copies.append(
-                remote(pgt.at[h, m], pgr.at[h, :, own], psend.at[h], precv.at[h], to)
-            )
-        seven = pgt.at[h, pl.ds(0, 7)]
-        a_copies[h] = post.together(
-            copies, remote(seven, seven, psend.at[h], precv.at[h], sib)
-        )
         pgr[h, :, own] = pgt[h, gy]
+        if h == 0:
+            exchange(0)
+            ngb[...] = backward(0)
 
     phase("normed_grad")
-    ngb[...] = lax.dot_general(
-        pg[...], win[...], (((1,), (1,)), ((), ())), preferred_element_type=F32
-    )
-
-    phase("ni_wait")
-    post.arrive(ni_copies)
-    pieces = [niall.at[2 * k + core] for k in range(4)]
-    four = niall.at[pl.ds(0, 4)]
-    f_copies = post.together(
-        [remote(p, p, fsend, frecv, sib) for p in pieces],
-        remote(four, four, fsend, frecv, sib),
-    )
-
+    ngb[...] = ngb[...] + backward(1)
+    exchange(1)
     phase("norm_grad")
 
     def norm_grad(r, sums):
@@ -518,23 +525,42 @@
                 red[pl.ds(base + a * 8 + b, 1), :] = jnp.sum(s, axis=0, keepdims=True)
         return 0
 
-    lax.fori_loop(0, CT, kernel_tile, 0)
     for t in range(CT):
         red[56 * t + 7 : 56 * t + 8, :] = gain_part[:, 128 * t : 128 * t + 128]
         red[56 * t + 15 : 56 * t + 16, :] = shift_part[:, 128 * t : 128 * t + 128]
 
-    def piece(m, yy):
-        return pl.ds(pl.multiple_of(m * 64 + yy * 16, 8), 16)
-
-    mine = piece(gx, y)
-    place = gx * 4 + y
-    copies = []
-    for iy, i in layer:
-        to, m, yy = in_layer(iy, i)
-        copies.append(remote(red.at[piece(m, yy)], redr.at[place], rsend, rrecv, to))
-    most = redr.at[pl.ds(0, 31)]
-    r_copies = post.together(copies, remote(most, most, rsend, rrecv, sib))
-    redr[place] = red[mine, :]
+    def share(m):
+        return pl.ds(pl.multiple_of(m * 64, 8), 64)
+
+    adds = gx < 6
+    rest = jnp.logical_not(adds)
+
+    def scatter(low, high):
+        for i in range(1, 8):
+            m = lax.rem(gx + i, 8)
+            copy = remote(red.at[share(m)], redr.at[gx], rsend, rrecv, in_gx(i))
+            pl.when((m >= low) & (m < high))(copy.start)
+
+    lax.fori_loop(0, 4, kernel_tile, 0)
+    scatter(0, 3)
+    lax.fori_loop(4, CT, kernel_tile, 0)
+    scatter(3, 6)
+    sizes = [redr.at[pl.ds(0, k)] for k in (5, 6, 7)]
+    five, six, seven = [remote(v, v, rsend, rrecv, sib) for v in sizes]
+    r_copies = post.partly([(five, adds), (six, rest)], [(seven, adds)])
+
+    @pl.when(adds)
+    def _():
+        redr[gx] = red[share(gx), :]
+
+    phase("ni_wait")
+    post.arrive(ni_copies)
+    pieces = [niall.at[2 * k + core] for k in range(4)]
+    four = niall.at[pl.ds(0, 4)]
+    f_copies = post.together(
+        [remote(p, p, fsend, frecv, sib) for p in pieces],
+        remote(four, four, fsend, frecv, sib),
+    )
 
     x_copies = [[], []]
 
@@ -600,45 +626,69 @@
             sx[r, :, at] = (out[r] + up[r, :, at].astype(F32)).astype(BF16)
         return 0
 
-    lax.fori_loop(0, CT, back_tile, 0)
-    og[...] = sx[:, :, 0:C]
-    o_copy = remote(og, ig_ref, osend.at[0], orecv.at[0], swap_dev)
-    o_local = pltpu.make_async_copy(og, ig_ref, lsem.at[0])
-
-    post.send(o_copy, swap, swap)
-    post.move(o_local, jnp.logical_not(swap))
-    weight(1)
+    o_copies, o_locals = [], []
+    for k in range(3):
+        lax.fori_loop(k * CT // 3, (k + 1) * CT // 3, back_tile, 0)
+        n = min(256, C - 256 * k)
+        at = pl.ds(256 * k, n)
+        og[:, :, 256 * k : 256 * k + n] = sx[:, :, 256 * k : 256 * k + n]
+        src, dst = og.at[:, :, at], ig_ref.at[:, :, at]
+        copy = remote(src, dst, osend.at[k], orecv.at[k], swap_dev)
+        o_copies.append(post.send(copy, swap, swap))
+        copy = pltpu.make_async_copy(src, dst, lsem.at[2 + k])
+        o_locals.append(post.move(copy, jnp.logical_not(swap)))
 
     phase("r_wait")
     post.arrive(r_copies)
-    total = redr[0]
-    for i in range(1, 32):
-        total = total + redr[i]
-    zsum[...] = total
-    seven = zar.at[pl.ds(0, 7)]
-    s_copies = post.together(
-        [remote(zsum, zar.at[z], asend, arecv, in_z(i)) for i in range(1, 8)],
-        remote(seven, seven, asend, arecv, sib),
-    )
-    zar[z] = total
+    three = remote(yr.at[pl.ds(0, 3)], yr.at[pl.ds(0, 3)], ysend, yrecv, sib)
+    y_copies = post.partly([(three, adds)], [(three, adds)])
+
+    @pl.when(adds)
+    def _():
+        total = redr[0]
+        for i in range(1, 8):
+            total = total + redr[i]
+        ysum[...] = total.reshape(4, 16, 128)
+        for i in range(1, 4):
+            k = lax.rem(y + i, 4)
+            remote(ysum.at[k], yr.at[y], ysend, yrecv, dev(y=k)).start()
+        yr[y] = ysum[y]
+
+    weight(1)
+    phase("y_wait")
+    post.arrive(y_copies)
+    seven = remote(zar.at[pl.ds(0, 7)], zar.at[pl.ds(0, 7)], asend, arecv, sib)
+    s_copies = post.partly([(seven, adds)], [(seven, adds)])
+
+    @pl.when(adds)
+    def _():
+        zsum[...] = yr[0] + yr[1] + yr[2] + yr[3]
+        for i in range(1, 8):
+            remote(zsum, zar.at[z], asend, arecv, in_z(i)).start()
+        zar[z] = zsum[...]
 
     shares(0)
+    shares(1)
 
     phase("s_wait")
     post.arrive(s_copies)
-    total = zar[0]
-    for i in range(1, 8):
-        total = total + zar[i]
-    back[...] = total
-    l_copies = post.together(
-        [
-            remote(back, fin.at[mine], qsend, qrecv, in_layer(iy, i)[0])
-            for iy, i in layer
-        ],
-        remote(most, most, qsend, qrecv, sib),
-    )
-    own_sums = post.move(pltpu.make_async_copy(back, fin.at[mine], lsem.at[1]))
-    shares(1)
+    mine = pl.ds(pl.multiple_of(gx * 64 + y * 16, 8), 16)
+    sizes = [red.at[pl.ds(0, 16 * k)] for k in (31, 23, 24)]
+    sent, more, all_of = [remote(v, v, qsend, qrecv, sib) for v in sizes]
+    l_copies = post.partly([(sent, adds)], [(more, adds), (all_of, rest)])
+    own_sums = pltpu.make_async_copy(back, fin.at[mine], lsem.at[1])
+
+    @pl.when(adds)
+    def _():
+        total = zar[0]
+        for i in range(1, 8):
+            total = total + zar[i]
+        back[...] = total
+        for iy, i in layer:
+            remote(back, fin.at[mine], qsend, qrecv, in_layer(iy, i)[0]).start()
+        own_sums.start()
+
+    post.inside.append((own_sums, adds))
     seven = zs.at[pl.ds(0, 7)]
     z_comes = post.together([], remote(seven, seven, zsend, zrecv, sib))
     phase("z_wait")
@@ -646,8 +696,8 @@
     phase("l_wait")
     post.arrive(l_copies)
     phase("o_wait")
-    post.arrive([o_copy])
-    post.moved([o_local, own_sums])
+    post.arrive(o_copies)
+    post.moved(o_locals + [own_sums])
     pltpu.make_async_copy(zs.at[0], zr.at[z], zlocal).wait()
 
     phase("sends")
@@ -727,7 +777,9 @@
         pltpu.VMEM((T, CP), F32),
         pltpu.VMEM((R + 6, W, 128), F32),
         pltpu.VMEM((512, 128), F32),
-        pltpu.VMEM((32, 16, 128), F32),
+        pltpu.VMEM((8, 64, 128), F32),
+        pltpu.VMEM((4, 16, 128), F32),
+        pltpu.VMEM((4, 16, 128), F32),
         pltpu.VMEM((16, 128), F32),
         pltpu.VMEM((8, 16, 128), F32),
         pltpu.VMEM((16, 128), F32),
@@ -739,14 +791,15 @@
         dma, dma,
         dma, dma,
         dma((2,)), dma((2,)),
-        dma((2,)),
+        dma((5,)),
         dma((2,)), dma((2,)),
+        dma, dma,
         dma, dma,
         dma, dma,
         dma,
         dma, dma,
         dma, dma,
-        dma((1,)), dma((1,)),
+        dma((3,)), dma((3,)),
     ]
     outs = pl.pallas_call(
         body,

time: 62 us -> 60.1 us (0.969)
  Pallas kernels: 61.2 us -> 59.3 us
    pallas_call x1, Pallas kernels: 59.2 us -> 57.3 us  [shards(): pl.pallas_call(body, out_shape=(jax.ShapeDtypeStruct((R, W, C), BF16), ja...]
where the time goes in v4:
time: 60.1 us; the launch traced here: 60 us
  Pallas kernels  59.3 us (99%)
  between operations  0.64 us (1%)
    pallas_call x1, Pallas kernels, shards(): pl.pallas_call(body, out_shape=(jax.ShapeDtypeStruct((R, W, C), BF16), ja...  57.3 us
    pallas_call x1, Pallas kernels, shards(): pl.pallas_call(finish, out_shape=(jax.ShapeDtypeStruct((R, W, C), BF16),...  1.98 us

profile of v4, /device:TPU:1, one launch (start us, length us, event | category | flops | bytes accessed | tf_op | source)
XLA Modules:
  0.0 60.0 jit_solution(4743562035610897465)
XLA Ops:
  0.6 57.3 %shard_map.155 = (bf16[4,32,704]{2,1,0:T(8,128)(2,1)}, bf16[8,16,768]{2,1,0:T(8,128)(2,1)}, f32[512,128]{1,0:T(8,128)}) custom-call(bf16[4,32,704]{2,1,0:T(8,128)(2,1)} %bitcast.15, s32[22,4,32]{2,1,0:T(4,128)} %bitcast.17, bf16[4,32,704]{2,1,0:T(8,128)(2,1)} %bitcast.16, s32[22,4,32]{2,1,0:T(4,128)} %bitcast.18, f32[7,7,704]{2,1,0:T(8,128)} %ck_in.1, ...), custom_call_target="tpu_custom_call" | custom-call | tf_op jit(solution)/shard_map/pallas_call | solution.py:804
  58.0 2.0 %shard_map.156 = (bf16[4,32,704]{2,1,0:T(8,128)(2,1)}, f32[11,704]{1,0:T(8,128)}, f32[7,7,704]{2,1,0:T(8,128)}, f32[2,704]{1,0:T(2,128)}, f32[2,2816]{1,0:T(2,128)}) custom-call(bf16[4,32,704]{2,1,0:T(8,128)(2,1)} %get-tuple-element.13.ig_ref, bf16[8,16,768]{2,1,0:T(8,128)(2,1)} %get-tuple-element.14.zr, f32[512,128]{1,0:T(8,128)} %get-tuple-element.15.fin), custom_call_target="tpu_custom_call" | custom-call | tf_op jit(solution)/shard_map/pallas_call | solution.py:831

commit v5 on v4

--- a/solution.py
+++ b/solution.py
@@ -269,7 +269,8 @@
     ]
     swap_u = remote(su, up, ssend.at[3], srecv.at[3], swap_dev)
 
-    post.send(swap_x[0], swap, swap)
+    for c in swap_x:
+        post.send(c, swap, swap)
     post.moved(loads[2:])
     scaled(grad_ref, gexp_ref, su)
 
@@ -324,13 +325,10 @@
     for k in range(4):
         if k < 3:
             phase("swap_wait%d" % k)
-            post.left([swap_x[k]])
-            if k < 2:
-                post.send(swap_x[k + 1], swap, swap)
-            else:
-                post.send(swap_u, swap, swap)
             post.arrive([swap_x[k]])
             near.append(halo(xs, 2 * k, thirds[k]))
+        if k == 2:
+            post.send(swap_u, swap, swap)
         if k > 0:
             phase("halo_wait%d" % (k - 1))
             post.arrive(near[k - 1])
@@ -626,6 +624,7 @@
             sx[r, :, at] = (out[r] + up[r, :, at].astype(F32)).astype(BF16)
         return 0
 
+    post.left(swap_x)
     o_copies, o_locals = [], []
     for k in range(3):
         lax.fori_loop(k * CT // 3, (k + 1) * CT // 3, back_tile, 0)

time: 60.1 us -> 60.6 us (level)
  no operation moved by 1% of the time
where the time goes in v5:
time: 60.6 us; the launch traced here: 60.5 us
  Pallas kernels  59.9 us (99%)
  between operations  0.64 us (1%)
    pallas_call x1, Pallas kernels, shards(): pl.pallas_call(body, out_shape=(jax.ShapeDtypeStruct((R, W, C), BF16), ja...  57.9 us
    pallas_call x1, Pallas kernels, shards(): pl.pallas_call(finish, out_shape=(jax.ShapeDtypeStruct((R, W, C), BF16),...  1.98 us

profile of v5, /device:TPU:1, one launch (start us, length us, event | category | flops | bytes accessed | tf_op | source)
XLA Modules:
  0.0 60.5 jit_solution(9661179120786143479)
XLA Ops:
  0.6 57.9 %shard_map.155 = (bf16[4,32,704]{2,1,0:T(8,128)(2,1)}, bf16[8,16,768]{2,1,0:T(8,128)(2,1)}, f32[512,128]{1,0:T(8,128)}) custom-call(bf16[4,32,704]{2,1,0:T(8,128)(2,1)} %bitcast.15, s32[22,4,32]{2,1,0:T(4,128)} %bitcast.17, bf16[4,32,704]{2,1,0:T(8,128)(2,1)} %bitcast.16, s32[22,4,32]{2,1,0:T(4,128)} %bitcast.18, f32[7,7,704]{2,1,0:T(8,128)} %ck_in.1, ...), custom_call_target="tpu_custom_call" | custom-call | tf_op jit(solution)/shard_map/pallas_call | solution.py:803
  58.5 2.0 %shard_map.156 = (bf16[4,32,704]{2,1,0:T(8,128)(2,1)}, f32[11,704]{1,0:T(8,128)}, f32[7,7,704]{2,1,0:T(8,128)}, f32[2,704]{1,0:T(2,128)}, f32[2,2816]{1,0:T(2,128)}) custom-call(bf16[4,32,704]{2,1,0:T(8,128)(2,1)} %get-tuple-element.13.ig_ref, bf16[8,16,768]{2,1,0:T(8,128)(2,1)} %get-tuple-element.14.zr, f32[512,128]{1,0:T(8,128)} %get-tuple-element.15.fin), custom_call_target="tpu_custom_call" | custom-call | tf_op jit(solution)/shard_map/pallas_call | solution.py:830
